TPU v7x, 256 devices: a whole 4x4x8 slice. The times are simulated.
256 devices in a mesh: dp: 32 (over z_lo, x, core), tensor: 8 (over y, z_hi).
Axes of the slice: x: 4, y: 4, z: 8 (z_hi: 2, z_lo: 4; z = z_hi * 4 + z_lo), core: 2. Of those that a mesh axis runs over, the one named last changes fastest.
Arguments:
- inputs: bfloat16 [768, 8192], P('dp', 'tensor'), may hold values from -6 to 6
- grad_out: bfloat16 [768, 8192], P('dp', 'tensor'), may hold values from -6 to 6
- w_gate: bfloat16 [8192, 28672], P('tensor', 'dp'), may hold values from -0.0625 to 0.0625
- w_up: bfloat16 [8192, 28672], P('tensor', 'dp'), may hold values from -0.0625 to 0.0625
- w_down: bfloat16 [28672, 8192], P('dp', 'tensor'), may hold values from -0.03125 to 0.03125
Outputs:
- grad_in: bfloat16 [768, 8192], P('dp', 'tensor')
- grad_gate: bfloat16 [8192, 28672], P('tensor', 'dp')
- grad_up: bfloat16 [8192, 28672], P('tensor', 'dp')
- grad_down: bfloat16 [28672, 8192], P('dp', 'tensor')
All inputs are finite; a program needn't handle non-finite values.
Results may differ from a plain program's by a relative error of at most 0.0049.
Values may be sent and summed in bfloat16 or wider, within the bound.
No kernel may reach another device: no remote copies, remote signals or barrier semaphores. Data moves between devices by JAX's collectives and lax.ppermute only.
A program may use at most 128 MiB of HBM per device.

v0:
```python
import jax
import jax.numpy as jnp
from jax import lax
from jax.sharding import PartitionSpec as P


def swiglu_grads(gate_pre, up_pre, hid_grad):
    sig_gate = jax.nn.sigmoid(gate_pre)
    silu_gate = gate_pre * sig_gate
    hidden = (silu_gate * up_pre).astype(jnp.bfloat16)
    gate_grad = (hid_grad * up_pre * sig_gate * (1.0 + gate_pre * (1.0 - sig_gate))).astype(
        jnp.bfloat16
    )
    up_grad = (hid_grad * silu_gate).astype(jnp.bfloat16)
    return (hidden, gate_grad, up_grad)


def contract_rows(left, right):
    return lax.dot_general(
        left, right, (((0,), (0,)), ((), ())), preferred_element_type=jnp.float32
    )


def contract_cols(left, right):
    return lax.dot_general(
        left, right, (((1,), (1,)), ((), ())), preferred_element_type=jnp.float32
    )


def body(inputs, grad_out, w_gate, w_up, w_down):
    rows_all, grads_all = (
        lax.all_gather(inputs, "dp", axis=0, tiled=True),
        lax.all_gather(grad_out, "dp", axis=0, tiled=True),
    )
    gate_part = jnp.dot(rows_all, w_gate, preferred_element_type=jnp.float32)
    up_part = jnp.dot(rows_all, w_up, preferred_element_type=jnp.float32)
    hid_part = contract_cols(grads_all, w_down)
    stacked = jnp.stack([gate_part, up_part, hid_part])
    shares = lax.psum_scatter(stacked, "tensor", scatter_dimension=1, tiled=True)
    local_hidden, local_gate, local_up = swiglu_grads(shares[0], shares[1], shares[2])
    packed = jnp.stack([local_hidden, local_gate, local_up])
    gathered = lax.all_gather(packed, "tensor", axis=1, tiled=True)
    hidden, gate_grad, up_grad = (gathered[0], gathered[1], gathered[2])
    grad_gate = contract_rows(rows_all, gate_grad).astype(jnp.bfloat16)
    grad_up = contract_rows(rows_all, up_grad).astype(jnp.bfloat16)
    grad_down = contract_rows(hidden, grads_all).astype(jnp.bfloat16)
    grad_in = lax.psum_scatter(
        contract_cols(gate_grad, w_gate) + contract_cols(up_grad, w_up),
        "dp",
        scatter_dimension=0,
        tiled=True,
    ).astype(jnp.bfloat16)
    return (grad_in, grad_gate, grad_up, grad_down)


def solution(mesh):
    return jax.shard_map(
        body,
        mesh=mesh,
        in_specs=(
            P("dp", "tensor"),
            P("dp", "tensor"),
            P("tensor", "dp"),
            P("tensor", "dp"),
            P("dp", "tensor"),
        ),
        out_specs=(P("dp", "tensor"), P("tensor", "dp"), P("tensor", "dp"), P("dp", "tensor")),
        check_vma=False,
    )
```

profile of v0, /device:TPU:1, one launch (start us, length us, event | category | flops | bytes accessed | tf_op | source)
XLA Modules:
  0.0 582.7 jit_solution(16901895669728103381)
XLA Ops:
  7.2 0.7 all-gather.4.cloned.1.call-update
  8.0 0.7 all-gather.6.cloned.1.call-update
  8.7 0.0 reduce-scatter.3.cloned.1.call-start
  8.7 65.0 %all-gather.4.cloned.1.call-done = bf16[768,1024]{1,0:T(8,128)(2,1)} async-done(((bf16[24,1024]{1,0:T(8,128)(2,1)}), bf16[768,1024]{1,0:T(8,128)(2,1)}) %all-gather.4.cloned.1.call-update) | async-done | bytes 1572880 | tf_op jit(solution)/shard_map/all_gather | solution.py:32
  73.7 5.4 convolution_bitcast_fusion.1
  79.2 3.4 convolution_bitcast_fusion.2
  82.6 51.6 %all-gather.6.cloned.1.call-done = bf16[768,1024]{1,0:T(8,128)(2,1)} async-done(((bf16[24,1024]{1,0:T(8,128)(2,1)}), bf16[768,1024]{1,0:T(8,128)(2,1)}) %all-gather.6.cloned.1.call-update) | async-done | bytes 1572880 | tf_op jit(solution)/shard_map/all_gather | solution.py:33
  134.2 3.9 convolution_bitcast_fusion
  138.2 3.5 pad_maximum_fusion
  141.7 0.0 all-gather.8.cloned.1.call-start
  141.7 182.2 %reduce-scatter.3.cloned.1.call-done = f32[3,96,896]{2,1,0:T(8,128)} async-done(((f32[3,768,896]{2,1,0:T(8,128)}), f32[3,96,896]{2,1,0:T(8,128)}) %reduce-scatter.3.cloned.1.call-update) | async-done | bytes 1032208 | tf_op jit(solution)/shard_map/reduce_scatter | solution.py:39
  324.0 1.4 multiply_convert_fusion.2
  325.4 0.9 pad_maximum_fusion.1
  326.2 0.0 reduce-scatter.5.cloned.1.call-start
  326.3 102.0 %all-gather.8.cloned.1.call-done = bf16[3,768,896]{2,1,0:T(8,128)(2,1)} async-done(((bf16[3,96,896]{2,1,0:T(8,128)(2,1)}), bf16[3,768,896]{2,1,0:T(8,128)(2,1)}) %all-gather.8.cloned.1.call-update) | async-done | bytes 4128784 | tf_op jit(solution)/shard_map/all_gather | solution.py:42
  428.3 3.3 fusion
  431.6 4.9 convolution_add_fusion
  436.5 4.2 convert_bitcast_fusion
  440.7 3.8 copy.10
  444.5 4.2 convert_bitcast_fusion.1
  448.7 3.9 copy.9
  452.6 4.2 convolution_convert_fusion
  456.8 117.9 %reduce-scatter.5.cloned.1.call-done = f32[24,1024]{1,0:T(8,128)} async-done(((f32[768,1024]{1,0:T(8,128)}), f32[24,1024]{1,0:T(8,128)}) %reduce-scatter.5.cloned.1.call-update) | async-done | bytes 98320 | tf_op jit(solution)/shard_map/reduce_scatter | solution.py:47
  574.7 1.5 convert_element_type.33
  (17 shorter events, 0.2 us)
Async XLA Ops:
  7.2 72.0 %copy-start = (bf16[1024,896]{1,0:T(8,128)(2,1)S(1)}, bf16[1024,896]{1,0:T(8,128)(2,1)}, u32[]{:S(2)}) copy-start(bf16[1024,896]{1,0:T(8,128)(2,1)} %param.7) | copy-start | bytes 5505028
  7.2 66.6 %all-gather.4.cloned.1.call-start = ((), (), s32[]{:S(2)}) async-start(), calls=%async_computation.2 | async-start | bytes 1622016 | tf_op jit(solution)/shard_map/all_gather | solution.py:32
  7.9 126.3 %all-gather.6.cloned.1.call-start = ((), (), s32[]{:S(2)}) async-start(), calls=%async_computation.3 | async-start | bytes 1622016 | tf_op jit(solution)/shard_map/all_gather | solution.py:33
  8.7 315.3 %reduce-scatter.3.cloned.1.call-start = ((), (), s32[]{:S(2)}) async-start(), calls=%async_computation.4 | async-start | bytes 9289728 | tf_op jit(solution)/shard_map/reduce_scatter | solution.py:39
  73.7 5.4 copy-start.4
  134.2 4.0 copy-start.1
  134.2 4.0 copy-start.2
  141.7 286.6 %all-gather.8.cloned.1.call-start = ((), (), s32[]{:S(2)}) async-start(), calls=%async_computation.5 | async-start | bytes 4644864 | tf_op jit(solution)/shard_map/all_gather | solution.py:42
  326.2 248.4 %reduce-scatter.5.cloned.1.call-start = ((), (), s32[]{:S(2)}) async-start(), calls=%async_computation.6 | async-start | bytes 3244032 | tf_op jit(solution)/shard_map/reduce_scatter | solution.py:47
  428.3 3.3 copy-start.3
  448.7 3.9 copy-start.5
Sparse Core Ops, SparseCore 0:
  9.9 63.8 all-gather.3
  75.6 58.5 all-gather.5
  141.8 182.1 reduce-scatter.2
  327.4 100.8 all-gather.7
  436.6 138.0 reduce-scatter.4
where the time goes:
time: 588 us; the launch traced here: 583 us
  waiting for transfers between devices  520 us (88%)
  matrix products  33.5 us (6%)
  between operations  13.8 us (2%)
  local copies, waits for them, and re-layouts  7.75 us (1%)
  other arithmetic  7.24 us (1%)
    reduce_scatter x1, waiting for transfers between devices, body(): lax.psum_scatter(stacked, 'tensor', scatter_dimension=1, tiled=True)  182 us
    reduce_scatter x1, waiting for transfers between devices, body(): lax.psum_scatter(contract_cols(gate_grad, w_gate) + contract_cols(up_grad...  118 us
    all_gather x1, waiting for transfers between devices, body(): gathered = lax.all_gather(packed, 'tensor', axis=1, tiled=True)  102 us
    all_gather x1, waiting for transfers between devices, body(): lax.all_gather(inputs, 'dp', axis=0, tiled=True)  65 us
    all_gather x1, waiting for transfers between devices, body(): lax.all_gather(grad_out, 'dp', axis=0, tiled=True)  51.6 us
    dot_general x3, matrix products, contract_rows(): lax.dot_general(left, right, (((0,), (0,)), ((), ())), preferred_element_...  12.6 us
    dot_general x3, matrix products, contract_cols(): lax.dot_general(left, right, (((1,), (1,)), ((), ())), preferred_element_...  12.1 us
  transfers between devices with their start and end apart: 5, of which 5 were waited for; matrix products, arithmetic and copies ran while one was open for 5% of the time, Pallas kernels for 0%

commit v1 on v0

v1 whole, which is shorter than its diff:
```python
import functools

import jax
import jax.numpy as jnp
from jax import lax
from jax.experimental import pallas as pl
from jax.experimental.pallas import tpu as pltpu
from jax.sharding import PartitionSpec as P

AXES = ("dp", "tensor")
F32 = jnp.float32
BF16 = jnp.bfloat16
ROWS = 48
WIDE = 1024
HID = 896
MIB = 1 << 20


def device_index(z, x, core, y):
    return (((z % 4) * 4 + x) * 2 + core) * 8 + y * 2 + z // 4


def swap(value, partner):
    pairs = [
        (device_index(z, x, c, y), device_index(*partner(z, x, c, y)))
        for z in range(8)
        for x in range(4)
        for c in range(2)
        for y in range(4)
    ]
    return lax.ppermute(value, AXES, pairs)


def swap_y(value, mask):
    return swap(value, lambda z, x, c, y: (z, x, c, y ^ mask))


def swap_z(value, mask):
    return swap(value, lambda z, x, c, y: (z ^ mask, x, c, y))


def swap_core(value):
    return swap(value, lambda z, x, c, y: (z, x, c ^ 1, y))


def swap_x(value, slot):
    return swap(value, lambda z, x, c, y: (z, x ^ y ^ slot, c, y))


def call(kernel, outs, args, flops, vmem):
    size = sum(a.size * a.dtype.itemsize for a in args)
    size += sum(o.size * o.dtype.itemsize for o in outs)
    whole = pl.BlockSpec(memory_space=pltpu.VMEM)
    return pl.pallas_call(
        kernel,
        out_shape=outs,
        in_specs=[whole] * len(args),
        out_specs=[whole] * len(outs),
        compiler_params=pltpu.CompilerParams(vmem_limit_bytes=vmem * MIB),
        cost_estimate=pl.CostEstimate(flops=flops, bytes_accessed=size, transcendentals=0),
    )(*args)


def shape(*dims, dtype=BF16):
    return jax.ShapeDtypeStruct(dims, dtype)


def forward_kernel(b0, b1, b2, b3, w_gate, w_up, w_down, far, near, own):
    blocks = (b0, b1, b2, b3)
    xs = jnp.concatenate([b[0] for b in blocks], axis=0)
    gs = jnp.concatenate([b[1] for b in blocks], axis=0)
    for i, (left, w, dim) in enumerate(((xs, w_gate, 0), (xs, w_up, 0), (gs, w_down, 1))):
        out = lax.dot_general(
            left, w[...], (((1,), (dim,)), ((), ())), preferred_element_type=F32
        )
        far[0, i] = out[:ROWS].astype(BF16)
        far[1, i] = out[ROWS : 2 * ROWS].astype(BF16)
        near[i] = out[2 * ROWS : 3 * ROWS]
        own[i] = out[3 * ROWS :]


def forward(blocks, weights, mask):
    order = (mask, 2, mask ^ 2, 0)
    return call(
        forward_kernel,
        [
            shape(2, 3, ROWS, HID),
            shape(3, ROWS, HID, dtype=F32),
            shape(3, ROWS, HID, dtype=F32),
        ],
        [blocks[k] for k in order] + list(weights),
        2 * 3 * 4 * ROWS * WIDE * HID,
        32,
    )


def grads_kernel(total, other, out):
    gate, up, hid = (total[i] + other[i].astype(F32) for i in range(3))
    sig = jax.nn.sigmoid(gate)
    silu = gate * sig
    out[0] = (silu * up).astype(BF16)
    out[1] = (hid * up * sig * (1.0 + gate * (1.0 - sig))).astype(BF16)
    out[2] = (hid * silu).astype(BF16)


def reduce_and_gather(blocks, weights, mask):
    last = mask ^ 2
    far, near, own = forward(blocks, weights, mask)
    far = swap_y(far, mask)
    near = swap_y((near + far[1].astype(F32)).astype(BF16), last)
    total = own + far[0].astype(F32) + near.astype(F32)
    other = swap_z(total.astype(BF16), 4)
    (grads,) = call(grads_kernel, [shape(3, ROWS, HID)], [total, other], 20 * 3 * ROWS * HID, 8)
    pair = jnp.stack([grads, swap_y(grads, last)])
    return pair, swap_y(pair, mask)


def backward_kernel(order, pair, rest, w_gate, w_up, out):
    total = 0.0
    for i, w in ((1, w_gate), (2, w_up)):
        left = jnp.concatenate([pair[0, i], pair[1, i], rest[0, i], rest[1, i]], axis=0)
        total += lax.dot_general(
            left, w[...], (((1,), (1,)), ((), ())), preferred_element_type=F32
        )
    for k, slot in enumerate(order):
        out[slot] = total[k * ROWS : (k + 1) * ROWS]


def backward(grads, w_gate, w_up, order):
    (out,) = call(
        functools.partial(backward_kernel, order),
        [shape(4, ROWS, WIDE, dtype=F32)],
        [*grads, w_gate, w_up],
        2 * 2 * 4 * ROWS * WIDE * HID,
        24,
    )
    return out


def join_kernel(mine, theirs, *outs):
    for k, out in enumerate(outs):
        out[...] = (mine[k] + theirs[k]).astype(BF16)


def reduce_x(own, other, w_gate, w_up):
    theirs = swap_core(backward(other, w_gate, w_up, (0, 1, 3, 2)))
    mine = backward(own, w_gate, w_up, (0, 3, 1, 2))
    parts = call(join_kernel, [shape(ROWS, WIDE)] * 4, [mine, theirs], 4 * ROWS * WIDE, 8)
    total = None
    for slot, part in enumerate(parts):
        term = swap_x(part, slot).astype(F32)
        total = term if total is None else total + term
    return total


def dot(left, right):
    return lax.dot_general(
        left, right, (((0,), (0,)), ((), ())), preferred_element_type=F32
    ).astype(BF16)


def body(inputs, grad_out, w_gate, w_up, w_down):
    weights = (w_gate, w_up, w_down)
    block = jnp.stack([inputs, grad_out])
    near = jnp.concatenate([block, swap_z(block, 1)], axis=1)
    far = swap_z(near, 2)
    groups, tokens, gathered = [], [], []
    for column in (near, far):
        own = [swap_x(column, k) for k in range(4)]
        other = [swap_core(b) for b in own]
        groups.append((reduce_and_gather(own, weights, 1), reduce_and_gather(other, weights, 3)))
        tokens += [own[k] for k in (0, 3, 1, 2)] + [other[k] for k in (0, 1, 3, 2)]
        for pair, rest in groups[-1]:
            gathered += [pair[0], pair[1], rest[0], rest[1]]

    sums = [reduce_x(own, other, w_gate, w_up) for own, other in groups]
    mine = sums[0] + swap_z(sums[1], 2)
    grad_in = (mine[:24] + swap_z(mine[24:], 1)).astype(BF16)

    rows_all, grads_all = (jnp.concatenate([b[i] for b in tokens], axis=0) for i in range(2))
    hidden, gate_grad, up_grad = (
        jnp.concatenate([b[i] for b in gathered], axis=0) for i in range(3)
    )
    return grad_in, dot(rows_all, gate_grad), dot(rows_all, up_grad), dot(hidden, grads_all)


def solution(mesh):
    return jax.shard_map(
        body,
        mesh=mesh,
        in_specs=(
            P("dp", "tensor"),
            P("dp", "tensor"),
            P("tensor", "dp"),
            P("tensor", "dp"),
            P("dp", "tensor"),
        ),
        out_specs=(P("dp", "tensor"), P("tensor", "dp"), P("tensor", "dp"), P("dp", "tensor")),
        check_vma=False,
    )
```

time: 588 us -> 200 us (0.34)
  waiting for transfers between devices: 520 us -> 25.3 us
  starting transfers between devices: 0.2 us -> 144 us
  matrix products: 33.5 us -> 9.05 us
  Pallas kernels: 0 us -> 12.6 us
  between operations: 13.8 us -> 1.35 us
    reduce_scatter x2 -> x0, waiting for transfers between devices: 300 us -> none  [the longest x1 182 us: body(): lax.psum_scatter(stacked, 'tensor', scatter_dimension=1, tiled=True)]
    all_gather x3 -> x0, waiting for transfers between devices: 219 us -> none  [the longest x1 102 us: body(): gathered = lax.all_gather(packed, 'tensor', axis=1, tiled=True)]
    ppermute x0 -> x50, starting transfers between devices: none -> 144 us  [swap(): return lax.ppermute(value, AXES, pairs)]
    ppermute x0 -> x50, waiting for transfers between devices: none -> 25.3 us  [swap(): return lax.ppermute(value, AXES, pairs)]
    dot_general x8 -> x3, matrix products: 33.5 us -> 9.05 us  [dot(): lax.dot_general(left, right, (((0,), (0,)), ((), ())), preferred_element_...]
    pallas_call x0 -> x14, Pallas kernels: none -> 12.6 us  [call(): pl.pallas_call(kernel, out_shape=outs, in_specs=[whole] * len(args), out_...]
  transfers between devices with their start and end apart: 5 -> 50, of which waited for: 5 -> 9; matrix products, arithmetic and copies ran while one was open for 5% -> 5% of each run, Pallas kernels for 0% -> 6%
where the time goes in v1:
time: 200 us; the launch traced here: 199 us
  starting transfers between devices  144 us (72%)
  waiting for transfers between devices  25.3 us (13%)
  Pallas kernels  12.6 us (6%)
  matrix products  9.05 us (5%)
  local copies, waits for them, and re-layouts  3.72 us (2%)
  other arithmetic  3.36 us (2%)
    ppermute x50, starting transfers between devices, swap(): return lax.ppermute(value, AXES, pairs)  144 us
    ppermute x50, waiting for transfers between devices, swap(): return lax.ppermute(value, AXES, pairs)  25.3 us
    pallas_call x14, Pallas kernels, call(): pl.pallas_call(kernel, out_shape=outs, in_specs=[whole] * len(args), out_...  12.6 us
    dot_general x3, matrix products, dot(): lax.dot_general(left, right, (((0,), (0,)), ((), ())), preferred_element_...  9.05 us
  transfers between devices with their start and end apart: 50, of which 9 were waited for; matrix products, arithmetic and copies ran while one was open for 5% of the time, Pallas kernels for 6%

profile of v1, /device:TPU:1, one launch (start us, length us, event | category | flops | bytes accessed | tf_op | source)
XLA Modules:
  0.0 199.1 jit_solution(1597277038007804053)
XLA Ops:
  7.0 3.5 %collective-permute-start.24 = (bf16[2,48,1024]{2,1,0:T(8,128)(2,1)S(1)}, bf16[2,48,1024]{2,1,0:T(8,128)(2,1)S(1)}, u32[]{:S(2)}, u32[]{:S(2)}) collective-permute-start(bf16[2,48,1024]{2,1,0:T(8,128)(2,1)S(1)} %pad_maximum_fusion.4), channel_id=1, source_target_pairs={{0,128},{2,130},{4,132},{6,134},{8,136},{10,138},{12,140},{14,142}... | collective-permute-start | bytes 589832 | tf_op jit(solution)/shard_map/ppermute | solution.py:31
  11.2 4.4 %collective-permute-start.3 = (bf16[2,48,1024]{2,1,0:T(8,128)(2,1)S(1)}, bf16[2,48,1024]{2,1,0:T(8,128)(2,1)S(1)}, u32[]{:S(2)}, u32[]{:S(2)}) collective-permute-start(bf16[2,48,1024]{2,1,0:T(8,128)(2,1)S(1)} %pad_maximum_fusion.4), channel_id=1, source_target_pairs={{0,48},{2,34},{4,20},{6,6},{8,56},{10,42},{12,28},{14,14},{16,32},... | collective-permute-start | bytes 589832 | tf_op jit(solution)/shard_map/ppermute | solution.py:31
  20.9 4.4 %collective-permute-start.27 = (bf16[2,48,1024]{2,1,0:T(8,128)(2,1)S(1)}, bf16[2,48,1024]{2,1,0:T(8,128)(2,1)S(1)}, u32[]{:S(2)}, u32[]{:S(2)}) collective-permute-start(bf16[2,48,1024]{2,1,0:T(8,128)(2,1)S(1)} %collective-permute-done.24), channel_id=1, source_target_pairs={{0,48},{2,34},{4,20},{6,6},{8,56},{10,42},{12,28},{14,14},{16,32},... | collective-permute-start | bytes 589832 | tf_op jit(solution)/shard_map/ppermute | solution.py:31
  30.0 3.4 %collective-permute-start.13 = (bf16[2,48,1024]{2,1,0:T(8,128)(2,1)S(1)}, bf16[2,48,1024]{2,1,0:T(8,128)(2,1)S(1)}, u32[]{:S(2)}, u32[]{:S(2)}) collective-permute-start(bf16[2,48,1024]{2,1,0:T(8,128)(2,1)S(1)} %collective-permute-done.4.b3), channel_id=1, source_target_pairs={{0,8},{2,10},{4,12},{6,14},{8,0},{10,2},{12,4},{14,6},{16,24},{18,... | collective-permute-start | bytes 589832 | tf_op jit(solution)/shard_map/ppermute | solution.py:31
  55.5 5.0 %collective-permute-done.14 = bf16[2,3,48,896]{3,2,1,0:T(8,128)(2,1)S(1)} collective-permute-done((bf16[2,3,48,896]{3,2,1,0:T(8,128)(2,1)S(1)}, bf16[2,3,48,896]{3,2,1,0:T(8,128)(2,1)S(1)}, u32[]{:S(2)}, u32[]{:S(2)}) %collective-permute-start.14) | collective-permute-done | bytes 516128 | tf_op jit(solution)/shard_map/ppermute | solution.py:31
  63.8 2.8 %collective-permute-start.30 = (bf16[3,48,896]{2,1,0:T(8,128)(2,1)S(1)}, bf16[3,48,896]{2,1,0:T(8,128)(2,1)S(1)}, u32[]{:S(2)}, u32[]{:S(2)}) collective-permute-start(bf16[3,48,896]{2,1,0:T(8,128)(2,1)S(1)} %fusion.2), channel_id=1, source_target_pairs={{0,6},{2,4},{4,2},{6,0},{8,14},{10,12},{12,10},{14,8},{16,22},{18,... | collective-permute-start | bytes 774152 | tf_op jit(solution)/shard_map/ppermute | solution.py:31
  66.6 10.5 %collective-permute-done.6 = bf16[3,48,896]{2,1,0:T(8,128)(2,1)S(1)} collective-permute-done((bf16[3,48,896]{2,1,0:T(8,128)(2,1)S(1)}, bf16[3,48,896]{2,1,0:T(8,128)(2,1)S(1)}, u32[]{:S(2)}, u32[]{:S(2)}) %collective-permute-start.6) | collective-permute-done | bytes 258080 | tf_op jit(solution)/shard_map/ppermute | solution.py:31
  77.2 5.2 %collective-permute-start.7 = (bf16[3,48,896]{2,1,0:T(8,128)(2,1)S(1)}, bf16[3,48,896]{2,1,0:T(8,128)(2,1)S(1)}, u32[]{:S(2)}, u32[]{:S(2)}) collective-permute-start(bf16[3,48,896]{2,1,0:T(8,128)(2,1)S(1)} %get-tuple-element.46), channel_id=1, source_target_pairs={{0,1},{2,3},{4,5},{6,7},{8,9},{10,11},{12,13},{14,15},{16,17},{18,... | collective-permute-start | bytes 774152 | tf_op jit(solution)/shard_map/ppermute | solution.py:31
  83.9 4.8 %collective-permute-start.31 = (bf16[3,48,896]{2,1,0:T(8,128)(2,1)S(1)}, bf16[3,48,896]{2,1,0:T(8,128)(2,1)S(1)}, u32[]{:S(2)}, u32[]{:S(2)}) collective-permute-start(bf16[3,48,896]{2,1,0:T(8,128)(2,1)S(1)} %get-tuple-element.50), channel_id=1, source_target_pairs={{0,1},{2,3},{4,5},{6,7},{8,9},{10,11},{12,13},{14,15},{16,17},{18,... | collective-permute-start | bytes 774152 | tf_op jit(solution)/shard_map/ppermute | solution.py:31
  88.8 3.5 %collective-permute-start.8 = (bf16[3,48,896]{2,1,0:T(8,128)(2,1)S(1)}, bf16[3,48,896]{2,1,0:T(8,128)(2,1)S(1)}, u32[]{:S(2)}, u32[]{:S(2)}) collective-permute-start(bf16[3,48,896]{2,1,0:T(8,128)(2,1)S(1)} %shard_map.85), channel_id=1, source_target_pairs={{0,6},{2,4},{4,2},{6,0},{8,14},{10,12},{12,10},{14,8},{16,22},{18,... | collective-permute-start | bytes 774152 | tf_op jit(solution)/shard_map/ppermute | solution.py:31
  92.4 5.8 %collective-permute-start.40 = (bf16[3,48,896]{2,1,0:T(8,128)(2,1)S(1)}, bf16[3,48,896]{2,1,0:T(8,128)(2,1)S(1)}, u32[]{:S(2)}, u32[]{:S(2)}) collective-permute-start(bf16[3,48,896]{2,1,0:T(8,128)(2,1)S(1)} %get-tuple-element.48), channel_id=1, source_target_pairs={{0,1},{2,3},{4,5},{6,7},{8,9},{10,11},{12,13},{14,15},{16,17},{18,... | collective-permute-start | bytes 774152 | tf_op jit(solution)/shard_map/ppermute | solution.py:31
  103.0 10.7 %collective-permute-start.32 = (bf16[3,48,896]{2,1,0:T(8,128)(2,1)S(1)}, bf16[3,48,896]{2,1,0:T(8,128)(2,1)S(1)}, u32[]{:S(2)}, u32[]{:S(2)}) collective-permute-start(bf16[3,48,896]{2,1,0:T(8,128)(2,1)S(1)} %shard_map.92), channel_id=1, source_target_pairs={{0,6},{2,4},{4,2},{6,0},{8,14},{10,12},{12,10},{14,8},{16,22},{18,... | collective-permute-start | bytes 774152 | tf_op jit(solution)/shard_map/ppermute | solution.py:31
  114.2 8.3 %collective-permute-start.41 = (bf16[3,48,896]{2,1,0:T(8,128)(2,1)S(1)}, bf16[3,48,896]{2,1,0:T(8,128)(2,1)S(1)}, u32[]{:S(2)}, u32[]{:S(2)}) collective-permute-start(bf16[3,48,896]{2,1,0:T(8,128)(2,1)S(1)} %shard_map.95), channel_id=1, source_target_pairs={{0,2},{2,0},{4,6},{6,4},{8,10},{10,8},{12,14},{14,12},{16,18},{18,... | collective-permute-start | bytes 774152 | tf_op jit(solution)/shard_map/ppermute | solution.py:31
  122.7 3.3 %collective-permute-start.18 = (bf16[2,3,48,896]{3,2,1,0:T(8,128)(2,1)S(1)}, bf16[2,3,48,896]{3,2,1,0:T(8,128)(2,1)S(1)}, u32[]{:S(2)}, u32[]{:S(2)}) collective-permute-start(bf16[2,3,48,896]{3,2,1,0:T(8,128)(2,1)S(1)} %pad_maximum_fusion.1.pair), channel_id=1, source_target_pairs={{0,6},{2,4},{4,2},{6,0},{8,14},{10,12},{12,10},{14,8},{16,22},{18,... | collective-permute-start | bytes 1548296 | tf_op jit(solution)/shard_map/ppermute | solution.py:31
  128.6 4.8 %collective-permute-start.42 = (bf16[2,3,48,896]{3,2,1,0:T(8,128)(2,1)S(1)}, bf16[2,3,48,896]{3,2,1,0:T(8,128)(2,1)S(1)}, u32[]{:S(2)}, u32[]{:S(2)}) collective-permute-start(bf16[2,3,48,896]{3,2,1,0:T(8,128)(2,1)S(1)} %pad_maximum_fusion.3.pair), channel_id=1, source_target_pairs={{0,6},{2,4},{4,2},{6,0},{8,14},{10,12},{12,10},{14,8},{16,22},{18,... | collective-permute-start | bytes 1548296 | tf_op jit(solution)/shard_map/ppermute | solution.py:31
  136.4 7.9 %collective-permute-start.19 = (f32[4,48,1024]{2,1,0:T(8,128)S(1)}, f32[4,48,1024]{2,1,0:T(8,128)S(1)}, u32[]{:S(2)}, u32[]{:S(2)}) collective-permute-start(f32[4,48,1024]{2,1,0:T(8,128)S(1)} %shard_map.89), channel_id=1, source_target_pairs={{0,8},{2,10},{4,12},{6,14},{8,0},{10,2},{12,4},{14,6},{16,24},{18,... | collective-permute-start | bytes 2359304 | tf_op jit(solution)/shard_map/ppermute | solution.py:31
  145.9 7.1 %collective-permute-start.43 = (f32[4,48,1024]{2,1,0:T(8,128)S(1)}, f32[4,48,1024]{2,1,0:T(8,128)S(1)}, u32[]{:S(2)}, u32[]{:S(2)}) collective-permute-start(f32[4,48,1024]{2,1,0:T(8,128)S(1)} %shard_map.96), channel_id=1, source_target_pairs={{0,8},{2,10},{4,12},{6,14},{8,0},{10,2},{12,4},{14,6},{16,24},{18,... | collective-permute-start | bytes 2359304 | tf_op jit(solution)/shard_map/ppermute | solution.py:31
  157.5 5.1 %collective-permute-start.46 = (bf16[48,1024]{1,0:T(8,128)(2,1)S(1)}, bf16[48,1024]{1,0:T(8,128)(2,1)S(1)}, u32[]{:S(2)}, u32[]{:S(2)}) collective-permute-start(bf16[48,1024]{1,0:T(8,128)(2,1)S(1)} %get-tuple-element.42), channel_id=1, source_target_pairs={{0,32},{2,50},{4,4},{6,22},{8,40},{10,58},{12,12},{14,30},{16,48},... | collective-permute-start | bytes 294920 | tf_op jit(solution)/shard_map/ppermute | solution.py:31
  165.2 3.1 %convolution_convert_fusion.1 = bf16[1024,896]{1,0:T(8,128)(2,1)} fusion(bf16[768,1024]{1,0:T(8,128)(2,1)S(1)} %get-tuple-element.101, bf16[768,896]{1,0:T(8,128)(2,1)S(1)} %get-tuple-element.53), kind=kOutput, calls=%fused_computation.1 | convolution fusion | flops 1410203648 | bytes 4784128 | tf_op jit(solution)/shard_map/dot_general | solution.py:157
  171.0 5.1 %collective-permute-start.22 = (bf16[48,1024]{1,0:T(8,128)(2,1)S(1)}, bf16[48,1024]{1,0:T(8,128)(2,1)S(1)}, u32[]{:S(2)}, u32[]{:S(2)}) collective-permute-start(bf16[48,1024]{1,0:T(8,128)(2,1)S(1)} %get-tuple-element.32), channel_id=1, source_target_pairs={{0,32},{2,50},{4,4},{6,22},{8,40},{10,58},{12,12},{14,30},{16,48},... | collective-permute-start | bytes 294920 | tf_op jit(solution)/shard_map/ppermute | solution.py:31
  178.8 6.9 %collective-permute-start.48 = (f32[48,1024]{1,0:T(8,128)S(1)}, f32[48,1024]{1,0:T(8,128)S(1)}, u32[]{:S(2)}, u32[]{:S(2)}) collective-permute-start(f32[48,1024]{1,0:T(8,128)S(1)} %convert_add_fusion.8), channel_id=1, source_target_pairs={{0,128},{2,130},{4,132},{6,134},{8,136},{10,138},{12,140},{14,142}... | collective-permute-start | bytes 589832 | tf_op jit(solution)/shard_map/ppermute | solution.py:31
  185.7 3.1 %convolution_convert_fusion.2 = bf16[1024,896]{1,0:T(8,128)(2,1)} fusion(bf16[768,1024]{1,0:T(8,128)(2,1)S(1)} %get-tuple-element.101, bf16[768,896]{1,0:T(8,128)(2,1)S(1)} %get-tuple-element.54), kind=kOutput, calls=%fused_computation.2 | convolution fusion | flops 1410203648 | bytes 4784128 | tf_op jit(solution)/shard_map/dot_general | solution.py:157
  189.2 6.5 %collective-permute-start.49 = (f32[24,1024]{1,0:T(8,128)S(1)}, f32[24,1024]{1,0:T(8,128)S(1)}, u32[]{:S(2)}, u32[]{:S(2)}) collective-permute-start(f32[24,1024]{1,0:T(8,128)S(1)} %slice.425), channel_id=1, source_target_pairs={{0,64},{2,66},{4,68},{6,70},{8,72},{10,74},{12,76},{14,78},{16,80}... | collective-permute-start | bytes 294920 | tf_op jit(solution)/shard_map/ppermute | solution.py:31
  195.6 2.9 %convolution_convert_fusion = bf16[896,1024]{1,0:T(8,128)(2,1)} fusion(bf16[768,896]{1,0:T(8,128)(2,1)S(1)} %get-tuple-element.52, bf16[768,1024]{1,0:T(8,128)(2,1)S(1)} %get-tuple-element.100), kind=kOutput, calls=%fused_computation | convolution fusion | flops 1410203648 | bytes 4784128 | tf_op jit(solution)/shard_map/dot_general | solution.py:157
  (151 shorter events, 70.1 us)
Async XLA Ops:
  20.2 17.8 %collective-permute-start.28 = (bf16[2,48,1024]{2,1,0:T(8,128)(2,1)S(1)}, bf16[2,48,1024]{2,1,0:T(8,128)(2,1)S(1)}, u32[]{:S(2)}, u32[]{:S(2)}) collective-permute-start(bf16[2,48,1024]{2,1,0:T(8,128)(2,1)S(1)} %collective-permute-done.24), channel_id=1, source_target_pairs={{0,0},{2,18},{4,36},{6,54},{8,8},{10,26},{12,44},{14,62},{16,16},{... | collective-permute-start | bytes 589832 | tf_op jit(solution)/shard_map/ppermute | solution.py:31
  20.9 19.7 %collective-permute-start.27 = (bf16[2,48,1024]{2,1,0:T(8,128)(2,1)S(1)}, bf16[2,48,1024]{2,1,0:T(8,128)(2,1)S(1)}, u32[]{:S(2)}, u32[]{:S(2)}) collective-permute-start(bf16[2,48,1024]{2,1,0:T(8,128)(2,1)S(1)} %collective-permute-done.24), channel_id=1, source_target_pairs={{0,48},{2,34},{4,20},{6,6},{8,56},{10,42},{12,28},{14,14},{16,32},... | collective-permute-start | bytes 589832 | tf_op jit(solution)/shard_map/ppermute | solution.py:31
  25.3 15.6 %collective-permute-start.26 = (bf16[2,48,1024]{2,1,0:T(8,128)(2,1)S(1)}, bf16[2,48,1024]{2,1,0:T(8,128)(2,1)S(1)}, u32[]{:S(2)}, u32[]{:S(2)}) collective-permute-start(bf16[2,48,1024]{2,1,0:T(8,128)(2,1)S(1)} %collective-permute-done.24), channel_id=1, source_target_pairs={{0,32},{2,50},{4,4},{6,22},{8,40},{10,58},{12,12},{14,30},{16,48},... | collective-permute-start | bytes 589832 | tf_op jit(solution)/shard_map/ppermute | solution.py:31
  48.7 15.0 %collective-permute-start.29 = (bf16[2,3,48,896]{3,2,1,0:T(8,128)(2,1)S(1)}, bf16[2,3,48,896]{3,2,1,0:T(8,128)(2,1)S(1)}, u32[]{:S(2)}, u32[]{:S(2)}) collective-permute-start(bf16[2,3,48,896]{3,2,1,0:T(8,128)(2,1)S(1)} %get-tuple-element.35), channel_id=1, source_target_pairs={{0,2},{2,0},{4,6},{6,4},{8,10},{10,8},{12,14},{14,12},{16,18},{18,... | collective-permute-start | bytes 1548296 | tf_op jit(solution)/shard_map/ppermute | solution.py:31
  50.9 31.4 %collective-permute-start.38 = (bf16[2,3,48,896]{3,2,1,0:T(8,128)(2,1)S(1)}, bf16[2,3,48,896]{3,2,1,0:T(8,128)(2,1)S(1)}, u32[]{:S(2)}, u32[]{:S(2)}) collective-permute-start(bf16[2,3,48,896]{3,2,1,0:T(8,128)(2,1)S(1)} %get-tuple-element.38), channel_id=1, source_target_pairs={{0,6},{2,4},{4,2},{6,0},{8,14},{10,12},{12,10},{14,8},{16,22},{18,... | collective-permute-start | bytes 1548296 | tf_op jit(solution)/shard_map/ppermute | solution.py:31
  52.7 24.3 %collective-permute-start.6 = (bf16[3,48,896]{2,1,0:T(8,128)(2,1)S(1)}, bf16[3,48,896]{2,1,0:T(8,128)(2,1)S(1)}, u32[]{:S(2)}, u32[]{:S(2)}) collective-permute-start(bf16[3,48,896]{2,1,0:T(8,128)(2,1)S(1)} %fusion.6), channel_id=1, source_target_pairs={{0,6},{2,4},{4,2},{6,0},{8,14},{10,12},{12,10},{14,8},{16,22},{18,... | collective-permute-start | bytes 774152 | tf_op jit(solution)/shard_map/ppermute | solution.py:31
  60.5 22.4 %collective-permute-start.15 = (bf16[3,48,896]{2,1,0:T(8,128)(2,1)S(1)}, bf16[3,48,896]{2,1,0:T(8,128)(2,1)S(1)}, u32[]{:S(2)}, u32[]{:S(2)}) collective-permute-start(bf16[3,48,896]{2,1,0:T(8,128)(2,1)S(1)} %fusion.4), channel_id=1, source_target_pairs={{0,2},{2,0},{4,6},{6,4},{8,10},{10,8},{12,14},{14,12},{16,18},{18,... | collective-permute-start | bytes 774152 | tf_op jit(solution)/shard_map/ppermute | solution.py:31
  63.8 20.0 %collective-permute-start.30 = (bf16[3,48,896]{2,1,0:T(8,128)(2,1)S(1)}, bf16[3,48,896]{2,1,0:T(8,128)(2,1)S(1)}, u32[]{:S(2)}, u32[]{:S(2)}) collective-permute-start(bf16[3,48,896]{2,1,0:T(8,128)(2,1)S(1)} %fusion.2), channel_id=1, source_target_pairs={{0,6},{2,4},{4,2},{6,0},{8,14},{10,12},{12,10},{14,8},{16,22},{18,... | collective-permute-start | bytes 774152 | tf_op jit(solution)/shard_map/ppermute | solution.py:31
  83.0 15.2 %collective-permute-start.16 = (bf16[3,48,896]{2,1,0:T(8,128)(2,1)S(1)}, bf16[3,48,896]{2,1,0:T(8,128)(2,1)S(1)}, u32[]{:S(2)}, u32[]{:S(2)}) collective-permute-start(bf16[3,48,896]{2,1,0:T(8,128)(2,1)S(1)} %get-tuple-element.44), channel_id=1, source_target_pairs={{0,1},{2,3},{4,5},{6,7},{8,9},{10,11},{12,13},{14,15},{16,17},{18,... | collective-permute-start | bytes 774152 | tf_op jit(solution)/shard_map/ppermute | solution.py:31
  83.9 18.9 %collective-permute-start.31 = (bf16[3,48,896]{2,1,0:T(8,128)(2,1)S(1)}, bf16[3,48,896]{2,1,0:T(8,128)(2,1)S(1)}, u32[]{:S(2)}, u32[]{:S(2)}) collective-permute-start(bf16[3,48,896]{2,1,0:T(8,128)(2,1)S(1)} %get-tuple-element.50), channel_id=1, source_target_pairs={{0,1},{2,3},{4,5},{6,7},{8,9},{10,11},{12,13},{14,15},{16,17},{18,... | collective-permute-start | bytes 774152 | tf_op jit(solution)/shard_map/ppermute | solution.py:31
  88.8 24.9 %collective-permute-start.8 = (bf16[3,48,896]{2,1,0:T(8,128)(2,1)S(1)}, bf16[3,48,896]{2,1,0:T(8,128)(2,1)S(1)}, u32[]{:S(2)}, u32[]{:S(2)}) collective-permute-start(bf16[3,48,896]{2,1,0:T(8,128)(2,1)S(1)} %shard_map.85), channel_id=1, source_target_pairs={{0,6},{2,4},{4,2},{6,0},{8,14},{10,12},{12,10},{14,8},{16,22},{18,... | collective-permute-start | bytes 774152 | tf_op jit(solution)/shard_map/ppermute | solution.py:31
  92.4 21.7 %collective-permute-start.40 = (bf16[3,48,896]{2,1,0:T(8,128)(2,1)S(1)}, bf16[3,48,896]{2,1,0:T(8,128)(2,1)S(1)}, u32[]{:S(2)}, u32[]{:S(2)}) collective-permute-start(bf16[3,48,896]{2,1,0:T(8,128)(2,1)S(1)} %get-tuple-element.48), channel_id=1, source_target_pairs={{0,1},{2,3},{4,5},{6,7},{8,9},{10,11},{12,13},{14,15},{16,17},{18,... | collective-permute-start | bytes 774152 | tf_op jit(solution)/shard_map/ppermute | solution.py:31
  98.4 24.2 %collective-permute-start.17 = (bf16[3,48,896]{2,1,0:T(8,128)(2,1)S(1)}, bf16[3,48,896]{2,1,0:T(8,128)(2,1)S(1)}, u32[]{:S(2)}, u32[]{:S(2)}) collective-permute-start(bf16[3,48,896]{2,1,0:T(8,128)(2,1)S(1)} %shard_map.88), channel_id=1, source_target_pairs={{0,2},{2,0},{4,6},{6,4},{8,10},{10,8},{12,14},{14,12},{16,18},{18,... | collective-permute-start | bytes 774152 | tf_op jit(solution)/shard_map/ppermute | solution.py:31
  103.0 22.9 %collective-permute-start.32 = (bf16[3,48,896]{2,1,0:T(8,128)(2,1)S(1)}, bf16[3,48,896]{2,1,0:T(8,128)(2,1)S(1)}, u32[]{:S(2)}, u32[]{:S(2)}) collective-permute-start(bf16[3,48,896]{2,1,0:T(8,128)(2,1)S(1)} %shard_map.92), channel_id=1, source_target_pairs={{0,6},{2,4},{4,2},{6,0},{8,14},{10,12},{12,10},{14,8},{16,22},{18,... | collective-permute-start | bytes 774152 | tf_op jit(solution)/shard_map/ppermute | solution.py:31
  113.8 19.7 %collective-permute-start.9 = (bf16[2,3,48,896]{3,2,1,0:T(8,128)(2,1)S(1)}, bf16[2,3,48,896]{3,2,1,0:T(8,128)(2,1)S(1)}, u32[]{:S(2)}, u32[]{:S(2)}) collective-permute-start(bf16[2,3,48,896]{3,2,1,0:T(8,128)(2,1)S(1)} %pad_maximum_fusion.pair), channel_id=1, source_target_pairs={{0,2},{2,0},{4,6},{6,4},{8,10},{10,8},{12,14},{14,12},{16,18},{18,... | collective-permute-start | bytes 1548296 | tf_op jit(solution)/shard_map/ppermute | solution.py:31
  126.0 18.4 %collective-permute-start.33 = (bf16[2,3,48,896]{3,2,1,0:T(8,128)(2,1)S(1)}, bf16[2,3,48,896]{3,2,1,0:T(8,128)(2,1)S(1)}, u32[]{:S(2)}, u32[]{:S(2)}) collective-permute-start(bf16[2,3,48,896]{3,2,1,0:T(8,128)(2,1)S(1)} %pad_maximum_fusion.2.pair), channel_id=1, source_target_pairs={{0,2},{2,0},{4,6},{6,4},{8,10},{10,8},{12,14},{14,12},{16,18},{18,... | collective-permute-start | bytes 1548296 | tf_op jit(solution)/shard_map/ppermute | solution.py:31
  128.6 15.9 %collective-permute-start.42 = (bf16[2,3,48,896]{3,2,1,0:T(8,128)(2,1)S(1)}, bf16[2,3,48,896]{3,2,1,0:T(8,128)(2,1)S(1)}, u32[]{:S(2)}, u32[]{:S(2)}) collective-permute-start(bf16[2,3,48,896]{3,2,1,0:T(8,128)(2,1)S(1)} %pad_maximum_fusion.3.pair), channel_id=1, source_target_pairs={{0,6},{2,4},{4,2},{6,0},{8,14},{10,12},{12,10},{14,8},{16,22},{18,... | collective-permute-start | bytes 1548296 | tf_op jit(solution)/shard_map/ppermute | solution.py:31
  136.4 31.9 %collective-permute-start.19 = (f32[4,48,1024]{2,1,0:T(8,128)S(1)}, f32[4,48,1024]{2,1,0:T(8,128)S(1)}, u32[]{:S(2)}, u32[]{:S(2)}) collective-permute-start(f32[4,48,1024]{2,1,0:T(8,128)S(1)} %shard_map.89), channel_id=1, source_target_pairs={{0,8},{2,10},{4,12},{6,14},{8,0},{10,2},{12,4},{14,6},{16,24},{18,... | collective-permute-start | bytes 2359304 | tf_op jit(solution)/shard_map/ppermute | solution.py:31
  155.6 15.4 %collective-permute-start.45 = (bf16[48,1024]{1,0:T(8,128)(2,1)S(1)}, bf16[48,1024]{1,0:T(8,128)(2,1)S(1)}, u32[]{:S(2)}, u32[]{:S(2)}) collective-permute-start(bf16[48,1024]{1,0:T(8,128)(2,1)S(1)} %get-tuple-element.41), channel_id=1, source_target_pairs={{0,16},{2,2},{4,52},{6,38},{8,24},{10,10},{12,60},{14,46},{16,0},{... | collective-permute-start | bytes 294920 | tf_op jit(solution)/shard_map/ppermute | solution.py:31
  157.5 18.6 %collective-permute-start.46 = (bf16[48,1024]{1,0:T(8,128)(2,1)S(1)}, bf16[48,1024]{1,0:T(8,128)(2,1)S(1)}, u32[]{:S(2)}, u32[]{:S(2)}) collective-permute-start(bf16[48,1024]{1,0:T(8,128)(2,1)S(1)} %get-tuple-element.42), channel_id=1, source_target_pairs={{0,32},{2,50},{4,4},{6,22},{8,40},{10,58},{12,12},{14,30},{16,48},... | collective-permute-start | bytes 294920 | tf_op jit(solution)/shard_map/ppermute | solution.py:31
  162.6 16.1 %collective-permute-start.47 = (bf16[48,1024]{1,0:T(8,128)(2,1)S(1)}, bf16[48,1024]{1,0:T(8,128)(2,1)S(1)}, u32[]{:S(2)}, u32[]{:S(2)}) collective-permute-start(bf16[48,1024]{1,0:T(8,128)(2,1)S(1)} %get-tuple-element.43), channel_id=1, source_target_pairs={{0,48},{2,34},{4,20},{6,6},{8,56},{10,42},{12,28},{14,14},{16,32},... | collective-permute-start | bytes 294920 | tf_op jit(solution)/shard_map/ppermute | solution.py:31
  168.4 20.4 %collective-permute-start.20 = (bf16[48,1024]{1,0:T(8,128)(2,1)S(1)}, bf16[48,1024]{1,0:T(8,128)(2,1)S(1)}, u32[]{:S(2)}, u32[]{:S(2)}) collective-permute-start(bf16[48,1024]{1,0:T(8,128)(2,1)S(1)} %get-tuple-element.30), channel_id=1, source_target_pairs={{0,0},{2,18},{4,36},{6,54},{8,8},{10,26},{12,44},{14,62},{16,16},{... | collective-permute-start | bytes 294920 | tf_op jit(solution)/shard_map/ppermute | solution.py:31
  169.1 19.7 %collective-permute-start.21 = (bf16[48,1024]{1,0:T(8,128)(2,1)S(1)}, bf16[48,1024]{1,0:T(8,128)(2,1)S(1)}, u32[]{:S(2)}, u32[]{:S(2)}) collective-permute-start(bf16[48,1024]{1,0:T(8,128)(2,1)S(1)} %get-tuple-element.31), channel_id=1, source_target_pairs={{0,16},{2,2},{4,52},{6,38},{8,24},{10,10},{12,60},{14,46},{16,0},{... | collective-permute-start | bytes 294920 | tf_op jit(solution)/shard_map/ppermute | solution.py:31
  171.0 17.8 %collective-permute-start.22 = (bf16[48,1024]{1,0:T(8,128)(2,1)S(1)}, bf16[48,1024]{1,0:T(8,128)(2,1)S(1)}, u32[]{:S(2)}, u32[]{:S(2)}) collective-permute-start(bf16[48,1024]{1,0:T(8,128)(2,1)S(1)} %get-tuple-element.32), channel_id=1, source_target_pairs={{0,32},{2,50},{4,4},{6,22},{8,40},{10,58},{12,12},{14,30},{16,48},... | collective-permute-start | bytes 294920 | tf_op jit(solution)/shard_map/ppermute | solution.py:31
  (30 other events, 293.9 us)

commit v2 on v0

v2 whole, which is shorter than its diff:
```python
import functools

import jax
import jax.numpy as jnp
from jax import lax
from jax.experimental import pallas as pl
from jax.experimental.pallas import tpu as pltpu
from jax.sharding import PartitionSpec as P

AXES = ("dp", "tensor")
F32 = jnp.float32
BF16 = jnp.bfloat16
PART = 24
ROWS = 4 * PART
WIDE = 1024
HID = 896
MIB = 1 << 20


def device_index(z, x, core, y):
    return (((z % 4) * 4 + x) * 2 + core) * 8 + y * 2 + z // 4


def swap(value, partner):
    pairs = [
        (device_index(z, x, c, y), device_index(*partner(z, x, c, y)))
        for z in range(8)
        for x in range(4)
        for c in range(2)
        for y in range(4)
    ]
    return lax.ppermute(value, AXES, pairs)


def swap_y(value, mask):
    return swap(value, lambda z, x, c, y: (z, x, c, y ^ mask))


def swap_z(value, mask):
    return swap(value, lambda z, x, c, y: (z ^ mask, x, c, y))


def swap_core(value):
    return swap(value, lambda z, x, c, y: (z, x, c ^ 1, y))


def swap_x(value, mask):
    return swap(value, lambda z, x, c, y: (z, x ^ mask, c, y))


VMEM = pl.BlockSpec(memory_space=pltpu.VMEM)
SMEM = pl.BlockSpec(memory_space=pltpu.SMEM)


def call(kernel, args, outs, vmem, later_than=(), y=None, scratch=(), flops=1):
    scalars = [] if y is None else [y]
    first, last = len(scalars), len(scalars) + len(args)

    def run(*refs):
        kernel(*refs[:last], *refs[last + len(later_than) :])

    return pl.pallas_call(
        run,
        out_shape=outs,
        in_specs=[SMEM] * first + [VMEM] * (len(args) + len(later_than)),
        out_specs=[VMEM] * len(outs),
        scratch_shapes=scratch,
        compiler_params=pltpu.CompilerParams(vmem_limit_bytes=vmem * MIB),
        cost_estimate=pl.CostEstimate(flops=flops, bytes_accessed=1, transcendentals=0),
    )(*scalars, *args, *later_than)


def shape(*dims, dtype=BF16):
    return jax.ShapeDtypeStruct(dims, dtype)


def touch_kernel(w_gate, w_up, out):
    out[...] = w_gate[:8, :128].astype(F32) + w_up[:8, :128].astype(F32)


def column_kernel(*refs):
    for i in range(4):
        refs[4][i * PART : (i + 1) * PART] = refs[i][...]


def products(tokens, weights, dims, sends, own):
    for i, (left, w, dim) in enumerate(zip(tokens, weights, dims)):
        out = lax.dot_general(
            left[...].reshape(4 * ROWS, WIDE),
            w[...],
            (((1,), (dim,)), ((), ())),
            preferred_element_type=F32,
        )
        for k, send in enumerate(sends):
            send[i] = out[(k + 1) * ROWS : (k + 2) * ROWS].astype(BF16)
        own[i] = out[:ROWS]


def gate_up_kernel(y_ref, *refs):
    blocks, weights, sends, own, xs = refs[:4], refs[4:6], refs[6:9], refs[9], refs[10]
    for j, block in enumerate(blocks):
        xs[j ^ y_ref[0]] = block[...]
    products((xs, xs), weights, (0, 0), sends, own)


def hid_kernel(y_ref, *refs):
    blocks, xs, w_down, sends, own, tokens = refs[:4], refs[4], refs[5], refs[6:9], refs[9], refs[10]
    tokens[0] = xs[...]
    for j, block in enumerate(blocks):
        tokens[1, j ^ y_ref[0]] = block[...]
    products((tokens.at[1],), (w_down,), (1,), sends, own)


def other_kernel(tokens, w_gate, w_up, w_down, *outs):
    left = (tokens.at[0], tokens.at[0], tokens.at[1])
    products(left, (w_gate, w_up, w_down), (0, 0, 1), outs[:3], outs[3])


def term_shapes(count):
    return [shape(count, ROWS, HID)] * 3 + [shape(count, ROWS, HID, dtype=F32)]


def total_kernel(*refs):
    terms, total, out = refs[:-2], refs[-2], refs[-1]
    at = 0
    for i in range(len(terms) // 4):
        own, *others = terms[i * 4 : (i + 1) * 4]
        value = own[...]
        for other in others:
            value += other[...].astype(F32)
        total[at : at + own.shape[0]] = value
        out[at : at + own.shape[0]] = value.astype(BF16)
        at += own.shape[0]


def total_step(terms, later_than=()):
    outs = [shape(3, ROWS, HID, dtype=F32), shape(3, ROWS, HID)]
    return call(total_kernel, terms, outs, 16, later_than)


def grads_kernel(total, other, out, hidden):
    gate, up, hid = (total[i] + other[i].astype(F32) for i in range(3))
    sig = jax.nn.sigmoid(gate)
    silu = gate * sig
    hidden[...] = (silu * up).astype(BF16)
    out[0] = (hid * up * sig * (1.0 + gate * (1.0 - sig))).astype(BF16)
    out[1] = (hid * silu).astype(BF16)


def grads_step(total, half, later_than):
    outs = [shape(2, ROWS, HID), shape(ROWS, HID)]
    return call(grads_kernel, [total, swap_z(half, 4)], outs, 16, later_than)


def swap_all_y(values):
    got = {k: swap_y(values[k - 1], k) for k in (2, 1, 3)}
    return [got[k] for k in (1, 2, 3)]


def backward_kernel(b0, b1, b2, b3, w_gate, w_up, out):
    total = 0.0
    for i, w in enumerate((w_gate, w_up)):
        left = jnp.concatenate([b[i] for b in (b0, b1, b2, b3)], axis=0)
        total += lax.dot_general(
            left, w[...], (((1,), (1,)), ((), ())), preferred_element_type=F32
        )
    for k in range(4):
        out[k] = total[k * ROWS : (k + 1) * ROWS]


def backward(blocks, w_gate, w_up, flops=1):
    outs = [shape(4, ROWS, WIDE, dtype=F32)]
    return call(backward_kernel, [*blocks, w_gate, w_up], outs, 12, flops=flops)[0]


def join_kernel(y_ref, mine, theirs, *outs):
    for j, out in enumerate(outs):
        slot = y_ref[0] ^ j
        out[...] = (mine[slot] + theirs[slot]).astype(out.dtype)


def sum_kernel(own, p1, p2, p3, *outs):
    value = own[...] + p1[...].astype(F32) + p2[...].astype(F32) + p3[...].astype(F32)
    for i, out in enumerate(outs):
        out[...] = value[i * PART : (i + 1) * PART]


def add_kernel(own, p1, p2, p3, out):
    out[...] = (own[...] + p1[...] + p2[...] + p3[...]).astype(BF16)


def reduce_tokens(y, mine, theirs, later_than):
    outs = [shape(ROWS, WIDE, dtype=F32)] + [shape(ROWS, WIDE)] * 3
    total, *parts = call(join_kernel, [mine, theirs], outs, 12, (), y)
    got = [swap_x(part, j + 1) for j, part in enumerate(parts)]
    sums = call(sum_kernel, [total, *got], [shape(PART, WIDE, dtype=F32)] * 4, 8, later_than)
    got = [swap_z(part, j + 1) for j, part in enumerate(sums[1:])]
    return call(add_kernel, [sums[0], *got], [shape(PART, WIDE)], 4)[0]


def rows_kernel(*refs):
    blocks, outs = refs[:8], refs[8:]
    for i, out in enumerate(outs):
        for k, block in enumerate(blocks):
            out[k * ROWS : (k + 1) * ROWS] = block[i]


def hidden_rows_kernel(*refs):
    blocks, out = refs[:4], refs[4]
    for group in range(2):
        for k, block in enumerate(blocks):
            at = (group * 4 + k) * ROWS
            out[at : at + ROWS] = block[group]


def stack_kernel(top, bottom, out):
    out[0] = top[...]
    out[1] = bottom[...]


def dot(left, right):
    return lax.dot_general(
        left, right, (((0,), (0,)), ((), ())), preferred_element_type=F32
    ).astype(BF16)


def gather_tokens(block, later_than=()):
    parts = [block] + [swap_z(block, j) for j in (1, 2, 3)]
    (column,) = call(column_kernel, parts, [shape(ROWS, WIDE)], 4, later_than)
    return [column] + [swap_x(column, j) for j in (1, 2, 3)]


def body(inputs, grad_out, w_gate, w_up, w_down):
    y = (lax.axis_index("tensor") // 2).astype(jnp.int32).reshape(1)
    ready = call(touch_kernel, [w_gate, w_up], [shape(8, 128, dtype=F32)], 8)
    xs = gather_tokens(inputs, ready)
    gs = gather_tokens(grad_out)

    outs = term_shapes(2) + [shape(4, ROWS, WIDE)]
    *sends, own, xs1 = call(gate_up_kernel, [*xs, w_gate, w_up], outs, 20, gs[:1], y)
    terms = [own, *swap_all_y(sends)]
    outs = term_shapes(1) + [shape(2, 4, ROWS, WIDE)]
    *sends, own, tokens1 = call(hid_kernel, [*gs, xs1, w_down], outs, 20, terms[1:], y)
    total1, half1 = total_step([*terms, own, *swap_all_y(sends)])
    tokens2 = swap_core(tokens1)
    args = [tokens2, w_gate, w_up, w_down]
    *sends, own = call(other_kernel, args, term_shapes(3), 20, [own])
    total2, half2 = total_step([own, *swap_all_y(sends)], [half1])

    grads1, hidden1 = grads_step(total1, half1, [half2])
    blocks1 = [grads1] + swap_all_y([grads1] * 3)
    grads2, hidden2 = grads_step(total2, half2, blocks1[1:])
    blocks2 = [grads2] + swap_all_y([grads2] * 3)
    mine = backward(blocks1, w_gate, w_up, 2 * 2 * 4 * ROWS * WIDE * HID)
    theirs = swap_core(backward(blocks2, w_gate, w_up))
    (hidden,) = call(stack_kernel, [hidden1, hidden2], [shape(2, ROWS, HID)], 4, blocks2[1:])
    hiddens = [hidden] + swap_all_y([hidden] * 3)

    rows = [shape(8 * ROWS, HID)]
    gate_grad, up_grad = call(rows_kernel, [*blocks1, *blocks2], rows * 2, 16)
    (hidden,) = call(hidden_rows_kernel, hiddens, rows, 12)
    xs, gs = (
        jnp.concatenate([t[i].reshape(4 * ROWS, WIDE) for t in (tokens1, tokens2)], axis=0)
        for i in range(2)
    )
    grad_gate, grad_up = dot(xs, gate_grad), dot(xs, up_grad)
    before = [grad_gate[:16, :128], grad_up[:16, :128], *hiddens[1:]]
    grad_in = reduce_tokens(y, mine, theirs, before)
    return grad_in, grad_gate, grad_up, dot(hidden, gs)


def solution(mesh):
    return jax.shard_map(
        body,
        mesh=mesh,
        in_specs=(
            P("dp", "tensor"),
            P("dp", "tensor"),
            P("tensor", "dp"),
            P("tensor", "dp"),
            P("dp", "tensor"),
        ),
        out_specs=(P("dp", "tensor"), P("tensor", "dp"), P("tensor", "dp"), P("dp", "tensor")),
        check_vma=False,
    )
```

time: 588 us -> 177 us (0.30)
  waiting for transfers between devices: 520 us -> 84.6 us
  starting transfers between devices: 0.2 us -> 65.1 us
  matrix products: 33.5 us -> 6.59 us
  between operations: 13.8 us -> 0.94 us
  Pallas kernels: 0 us -> 11.5 us
  other arithmetic: 7.24 us -> 0 us
    reduce_scatter x2 -> x0, waiting for transfers between devices: 300 us -> none  [the longest x1 182 us: body(): lax.psum_scatter(stacked, 'tensor', scatter_dimension=1, tiled=True)]
    all_gather x3 -> x0, waiting for transfers between devices: 219 us -> none  [the longest x1 102 us: body(): gathered = lax.all_gather(packed, 'tensor', axis=1, tiled=True)]
    ppermute x0 -> x40, waiting for transfers between devices: none -> 84.6 us  [swap(): return lax.ppermute(value, AXES, pairs)]
    ppermute x0 -> x40, starting transfers between devices: none -> 65.1 us  [swap(): return lax.ppermute(value, AXES, pairs)]
    dot_general x8 -> x3, matrix products: 33.5 us -> 6.59 us  [dot(): lax.dot_general(left, right, (((0,), (0,)), ((), ())), preferred_element_...]
    pallas_call x0 -> x18, Pallas kernels: none -> 11.5 us  [call(): pl.pallas_call(run, out_shape=outs, in_specs=[SMEM] * first + [VMEM] * (l...]
  transfers between devices with their start and end apart: 5 -> 40, of which waited for: 5 -> 24; matrix products, arithmetic and copies ran while one was open for 5% -> 4% of each run, Pallas kernels for 0% -> 4%
where the time goes in v2:
time: 177 us; the launch traced here: 175 us
  waiting for transfers between devices  84.6 us (48%)
  starting transfers between devices  65.1 us (37%)
  Pallas kernels  11.5 us (6%)
  matrix products  6.59 us (4%)
  local copies, waits for them, and re-layouts  5.88 us (3%)
    ppermute x40, waiting for transfers between devices, swap(): return lax.ppermute(value, AXES, pairs)  84.6 us
    ppermute x40, starting transfers between devices, swap(): return lax.ppermute(value, AXES, pairs)  65.1 us
    pallas_call x18, Pallas kernels, call(): pl.pallas_call(run, out_shape=outs, in_specs=[SMEM] * first + [VMEM] * (l...  11.5 us
    dot_general x3, matrix products, dot(): lax.dot_general(left, right, (((0,), (0,)), ((), ())), preferred_element_...  6.59 us
    unnamed x20, local copies, waits for them, and re-layouts  5.57 us
  transfers between devices with their start and end apart: 40, of which 24 were waited for; matrix products, arithmetic and copies ran while one was open for 4% of the time, Pallas kernels for 4%

profile of v2, /device:TPU:1, one launch (start us, length us, event | category | flops | bytes accessed | tf_op | source)
XLA Modules:
  0.0 174.6 jit_solution(6877432210972536188)
XLA Ops:
  0.6 2.6 %collective-permute-start = (bf16[24,1024]{1,0:T(8,128)(2,1)}, bf16[24,1024]{1,0:T(8,128)(2,1)S(1)}, u32[]{:S(2)}, u32[]{:S(2)}) collective-permute-start(bf16[24,1024]{1,0:T(8,128)(2,1)} %refs_0_.4), channel_id=1, source_target_pairs={{0,64},{2,66},{4,68},{6,70},{8,72},{10,74},{12,76},{14,78},{16,80}... | collective-permute-start | bytes 147464 | tf_op jit(solution)/shard_map/ppermute | solution.py:32
  3.2 3.0 %collective-permute-start.1 = (bf16[24,1024]{1,0:T(8,128)(2,1)}, bf16[24,1024]{1,0:T(8,128)(2,1)S(1)}, u32[]{:S(2)}, u32[]{:S(2)}) collective-permute-start(bf16[24,1024]{1,0:T(8,128)(2,1)} %refs_0_.4), channel_id=1, source_target_pairs={{0,128},{2,130},{4,132},{6,134},{8,136},{10,138},{12,140},{14,142}... | collective-permute-start | bytes 147464 | tf_op jit(solution)/shard_map/ppermute | solution.py:32
  20.4 2.9 %collective-permute-done.8.refs_3_ = bf16[24,1024]{1,0:T(8,128)(2,1)S(1)} collective-permute-done((bf16[24,1024]{1,0:T(8,128)(2,1)S(1)}, bf16[24,1024]{1,0:T(8,128)(2,1)S(1)}, u32[]{:S(2)}, u32[]{:S(2)}) %collective-permute-start.8) | collective-permute-done | bytes 49184 | tf_op jit(solution)/shard_map/ppermute | solution.py:32
  29.5 2.6 %collective-permute-start.10 = (bf16[2,96,896]{2,1,0:T(8,128)(2,1)S(1)}, bf16[2,96,896]{2,1,0:T(8,128)(2,1)S(1)}, u32[]{:S(2)}, u32[]{:S(2)}) collective-permute-start(bf16[2,96,896]{2,1,0:T(8,128)(2,1)S(1)} %get-tuple-element.38), channel_id=1, source_target_pairs={{0,4},{2,6},{4,0},{6,2},{8,12},{10,14},{12,8},{14,10},{16,20},{18,... | collective-permute-start | bytes 1032200 | tf_op jit(solution)/shard_map/ppermute | solution.py:32
  34.7 3.4 %collective-permute-done.13.refs_3_ = bf16[96,1024]{1,0:T(8,128)(2,1)S(1)} collective-permute-done((bf16[96,1024]{1,0:T(8,128)(2,1)S(1)}, bf16[96,1024]{1,0:T(8,128)(2,1)S(1)}, u32[]{:S(2)}, u32[]{:S(2)}) %collective-permute-start.13) | collective-permute-done | bytes 196640 | tf_op jit(solution)/shard_map/ppermute | solution.py:32
  40.3 3.4 %collective-permute-done.10.refs_8_.refs_2_ = bf16[2,96,896]{2,1,0:T(8,128)(2,1)S(1)} collective-permute-done((bf16[2,96,896]{2,1,0:T(8,128)(2,1)S(1)}, bf16[2,96,896]{2,1,0:T(8,128)(2,1)S(1)}, u32[]{:S(2)}, u32[]{:S(2)}) %collective-permute-start.10) | collective-permute-done | bytes 344096 | tf_op jit(solution)/shard_map/ppermute | solution.py:32
  45.7 6.7 %collective-permute-start.19 = (bf16[2,4,96,1024]{3,2,1,0:T(8,128)(2,1)S(1)}, bf16[2,4,96,1024]{3,2,1,0:T(8,128)(2,1)S(1)}, u32[]{:S(2)}, u32[]{:S(2)}) collective-permute-start(bf16[2,4,96,1024]{3,2,1,0:T(8,128)(2,1)S(1)} %get-tuple-element.47), channel_id=1, source_target_pairs={{0,8},{2,10},{4,12},{6,14},{8,0},{10,2},{12,4},{14,6},{16,24},{18,... | collective-permute-start | bytes 4718600 | tf_op jit(solution)/shard_map/ppermute | solution.py:32
  53.5 2.7 %collective-permute-start.17 = (bf16[1,96,896]{2,1,0:T(8,128)(2,1)S(1)}, bf16[1,96,896]{2,1,0:T(8,128)(2,1)S(1)}, u32[]{:S(2)}, u32[]{:S(2)}) collective-permute-start(bf16[1,96,896]{2,1,0:T(8,128)(2,1)S(1)} %get-tuple-element.44), channel_id=1, source_target_pairs={{0,6},{2,4},{4,2},{6,0},{8,14},{10,12},{12,10},{14,8},{16,22},{18,... | collective-permute-start | bytes 516104 | tf_op jit(solution)/shard_map/ppermute | solution.py:32
  56.2 2.6 %shard_map.90 = (bf16[3,96,896]{2,1,0:T(8,128)(2,1)S(1)}, bf16[3,96,896]{2,1,0:T(8,128)(2,1)S(1)}, bf16[3,96,896]{2,1,0:T(8,128)(2,1)S(1)}, f32[3,96,896]{2,1,0:T(8,128)S(1)}) custom-call(bf16[2,4,96,1024]{3,2,1,0:T(8,128)(2,1)S(1)} %collective-permute-done.19.refs_0_, bf16[1024,896]{1,0:T(8,128)(2,1)S(1)} %copy-done.1, bf16[1024,896]{1,0:T(8,128)(2,1)S(1)} %copy-done.4, ...), custom_call_target="tpu_custom_call" | custom-call | flops 1 | bytes 1 | tf_op jit(solution)/shard_map/pallas_call | solution.py:62
  60.1 2.7 %collective-permute-start.22 = (bf16[3,96,896]{2,1,0:T(8,128)(2,1)S(1)}, bf16[3,96,896]{2,1,0:T(8,128)(2,1)S(1)}, u32[]{:S(2)}, u32[]{:S(2)}) collective-permute-start(bf16[3,96,896]{2,1,0:T(8,128)(2,1)S(1)} %get-tuple-element.51), channel_id=1, source_target_pairs={{0,6},{2,4},{4,2},{6,0},{8,14},{10,12},{12,10},{14,8},{16,22},{18,... | collective-permute-start | bytes 1548296 | tf_op jit(solution)/shard_map/ppermute | solution.py:32
  64.3 5.3 %collective-permute-start.18 = (bf16[3,96,896]{2,1,0:T(8,128)(2,1)S(1)}, bf16[3,96,896]{2,1,0:T(8,128)(2,1)S(1)}, u32[]{:S(2)}, u32[]{:S(2)}) collective-permute-start(bf16[3,96,896]{2,1,0:T(8,128)(2,1)S(1)} %get-tuple-element.46.refs_4_), channel_id=1, source_target_pairs={{0,1},{2,3},{4,5},{6,7},{8,9},{10,11},{12,13},{14,15},{16,17},{18,... | collective-permute-start | bytes 1548296 | tf_op jit(solution)/shard_map/ppermute | solution.py:32
  69.6 3.4 %collective-permute-done.20.refs_1_ = bf16[3,96,896]{2,1,0:T(8,128)(2,1)S(1)} collective-permute-done((bf16[3,96,896]{2,1,0:T(8,128)(2,1)S(1)}, bf16[3,96,896]{2,1,0:T(8,128)(2,1)S(1)}, u32[]{:S(2)}, u32[]{:S(2)}) %collective-permute-start.20) | collective-permute-done | bytes 516128 | tf_op jit(solution)/shard_map/ppermute | solution.py:32
  72.9 10.8 %collective-permute-done.21.refs_2_ = bf16[3,96,896]{2,1,0:T(8,128)(2,1)S(1)} collective-permute-done((bf16[3,96,896]{2,1,0:T(8,128)(2,1)S(1)}, bf16[3,96,896]{2,1,0:T(8,128)(2,1)S(1)}, u32[]{:S(2)}, u32[]{:S(2)}) %collective-permute-start.21) | collective-permute-done | bytes 516128 | tf_op jit(solution)/shard_map/ppermute | solution.py:32
  86.0 5.3 %collective-permute-start.26 = (bf16[3,96,896]{2,1,0:T(8,128)(2,1)S(1)}, bf16[3,96,896]{2,1,0:T(8,128)(2,1)S(1)}, u32[]{:S(2)}, u32[]{:S(2)}) collective-permute-start(bf16[3,96,896]{2,1,0:T(8,128)(2,1)S(1)} %get-tuple-element.52.refs_2_), channel_id=1, source_target_pairs={{0,1},{2,3},{4,5},{6,7},{8,9},{10,11},{12,13},{14,15},{16,17},{18,... | collective-permute-start | bytes 1548296 | tf_op jit(solution)/shard_map/ppermute | solution.py:32
  91.6 3.8 %collective-permute-start.24 = (bf16[2,96,896]{2,1,0:T(8,128)(2,1)S(1)}, bf16[2,96,896]{2,1,0:T(8,128)(2,1)S(1)}, u32[]{:S(2)}, u32[]{:S(2)}) collective-permute-start(bf16[2,96,896]{2,1,0:T(8,128)(2,1)S(1)} %get-tuple-element.53.refs_0_), channel_id=1, source_target_pairs={{0,4},{2,6},{4,0},{6,2},{8,12},{10,14},{12,8},{14,10},{16,20},{18,... | collective-permute-start | bytes 1032200 | tf_op jit(solution)/shard_map/ppermute | solution.py:32
  95.5 3.8 %collective-permute-done.23.refs_1_.refs_2_ = bf16[2,96,896]{2,1,0:T(8,128)(2,1)S(1)} collective-permute-done((bf16[2,96,896]{2,1,0:T(8,128)(2,1)S(1)}, bf16[2,96,896]{2,1,0:T(8,128)(2,1)S(1)}, u32[]{:S(2)}, u32[]{:S(2)}) %collective-permute-start.23) | collective-permute-done | bytes 344096 | tf_op jit(solution)/shard_map/ppermute | solution.py:32
  99.3 9.8 %collective-permute-done.24.refs_2_.refs_3_ = bf16[2,96,896]{2,1,0:T(8,128)(2,1)S(1)} collective-permute-done((bf16[2,96,896]{2,1,0:T(8,128)(2,1)S(1)}, bf16[2,96,896]{2,1,0:T(8,128)(2,1)S(1)}, u32[]{:S(2)}, u32[]{:S(2)}) %collective-permute-start.24) | collective-permute-done | bytes 344096 | tf_op jit(solution)/shard_map/ppermute | solution.py:32
  109.1 8.6 %collective-permute-done.26.refs_1_ = bf16[3,96,896]{2,1,0:T(8,128)(2,1)S(1)} collective-permute-done((bf16[3,96,896]{2,1,0:T(8,128)(2,1)S(1)}, bf16[3,96,896]{2,1,0:T(8,128)(2,1)S(1)}, u32[]{:S(2)}, u32[]{:S(2)}) %collective-permute-start.26) | collective-permute-done | bytes 516128 | tf_op jit(solution)/shard_map/ppermute | solution.py:32
  118.1 3.8 %collective-permute-start.28 = (bf16[2,96,896]{2,1,0:T(8,128)(2,1)S(1)}, bf16[2,96,896]{2,1,0:T(8,128)(2,1)S(1)}, u32[]{:S(2)}, u32[]{:S(2)}) collective-permute-start(bf16[2,96,896]{2,1,0:T(8,128)(2,1)S(1)} %get-tuple-element.55.refs_0_.refs_4_), channel_id=1, source_target_pairs={{0,4},{2,6},{4,0},{6,2},{8,12},{10,14},{12,8},{14,10},{16,20},{18,... | collective-permute-start | bytes 1032200 | tf_op jit(solution)/shard_map/ppermute | solution.py:32
  121.9 4.9 %collective-permute-done.27.refs_1_.refs_5_.refs_2_ = bf16[2,96,896]{2,1,0:T(8,128)(2,1)S(1)} collective-permute-done((bf16[2,96,896]{2,1,0:T(8,128)(2,1)S(1)}, bf16[2,96,896]{2,1,0:T(8,128)(2,1)S(1)}, u32[]{:S(2)}, u32[]{:S(2)}) %collective-permute-start.27) | collective-permute-done | bytes 344096 | tf_op jit(solution)/shard_map/ppermute | solution.py:32
  126.8 9.8 %collective-permute-done.28.refs_2_.refs_6_.refs_3_ = bf16[2,96,896]{2,1,0:T(8,128)(2,1)S(1)} collective-permute-done((bf16[2,96,896]{2,1,0:T(8,128)(2,1)S(1)}, bf16[2,96,896]{2,1,0:T(8,128)(2,1)S(1)}, u32[]{:S(2)}, u32[]{:S(2)}) %collective-permute-start.28) | collective-permute-done | bytes 344096 | tf_op jit(solution)/shard_map/ppermute | solution.py:32
  146.6 2.7 %collective-permute-start.36 = (bf16[2,96,896]{2,1,0:T(8,128)(2,1)S(1)}, bf16[2,96,896]{2,1,0:T(8,128)(2,1)S(1)}, u32[]{:S(2)}, u32[]{:S(2)}) collective-permute-start(bf16[2,96,896]{2,1,0:T(8,128)(2,1)S(1)} %shard_map.98.refs_0_), channel_id=1, source_target_pairs={{0,6},{2,4},{4,2},{6,0},{8,14},{10,12},{12,10},{14,8},{16,22},{18,... | collective-permute-start | bytes 1032200 | tf_op jit(solution)/shard_map/ppermute | solution.py:32
  158.3 3.9 %collective-permute-done.35.refs_7_.refs_2_ = bf16[2,96,896]{2,1,0:T(8,128)(2,1)S(1)} collective-permute-done((bf16[2,96,896]{2,1,0:T(8,128)(2,1)S(1)}, bf16[2,96,896]{2,1,0:T(8,128)(2,1)S(1)}, u32[]{:S(2)}, u32[]{:S(2)}) %collective-permute-start.35) | collective-permute-done | bytes 344096 | tf_op jit(solution)/shard_map/ppermute | solution.py:32
  168.8 2.9 %convolution_convert_fusion = bf16[896,1024]{1,0:T(8,128)(2,1)} fusion(bf16[768,896]{1,0:T(8,128)(2,1)S(1)} %shard_map.101, bf16[384,1024]{1,0:T(8,128)(2,1)S(1)} %bitcast.9, bf16[384,1024]{1,0:T(8,128)(2,1)S(1)} %bitcast.8), kind=kOutput, calls=%fused_computation | convolution fusion | flops 1413349376 | bytes 4784128 | tf_op jit(solution)/shard_map/dot_general | solution.py:222
  (101 shorter events, 62.4 us)
Async XLA Ops:
  11.2 12.4 %collective-permute-start.3 = (bf16[96,1024]{1,0:T(8,128)(2,1)S(1)}, bf16[96,1024]{1,0:T(8,128)(2,1)S(1)}, u32[]{:S(2)}, u32[]{:S(2)}) collective-permute-start(bf16[96,1024]{1,0:T(8,128)(2,1)S(1)} %shard_map.85.refs_1_), channel_id=1, source_target_pairs={{0,16},{2,18},{4,20},{6,22},{8,24},{10,26},{12,28},{14,30},{16,0},... | collective-permute-start | bytes 589832 | tf_op jit(solution)/shard_map/ppermute | solution.py:32
  12.5 11.1 %collective-permute-start.4 = (bf16[96,1024]{1,0:T(8,128)(2,1)S(1)}, bf16[96,1024]{1,0:T(8,128)(2,1)S(1)}, u32[]{:S(2)}, u32[]{:S(2)}) collective-permute-start(bf16[96,1024]{1,0:T(8,128)(2,1)S(1)} %shard_map.85.refs_1_), channel_id=1, source_target_pairs={{0,32},{2,34},{4,36},{6,38},{8,40},{10,42},{12,44},{14,46},{16,48}... | collective-permute-start | bytes 589832 | tf_op jit(solution)/shard_map/ppermute | solution.py:32
  23.4 10.9 %collective-permute-start.12 = (bf16[96,1024]{1,0:T(8,128)(2,1)S(1)}, bf16[96,1024]{1,0:T(8,128)(2,1)S(1)}, u32[]{:S(2)}, u32[]{:S(2)}) collective-permute-start(bf16[96,1024]{1,0:T(8,128)(2,1)S(1)} %shard_map.86.refs_7_.refs_1_), channel_id=1, source_target_pairs={{0,16},{2,18},{4,20},{6,22},{8,24},{10,26},{12,28},{14,30},{16,0},... | collective-permute-start | bytes 589832 | tf_op jit(solution)/shard_map/ppermute | solution.py:32
  28.1 12.1 %collective-permute-start.9 = (bf16[2,96,896]{2,1,0:T(8,128)(2,1)S(1)}, bf16[2,96,896]{2,1,0:T(8,128)(2,1)S(1)}, u32[]{:S(2)}, u32[]{:S(2)}) collective-permute-start(bf16[2,96,896]{2,1,0:T(8,128)(2,1)S(1)} %get-tuple-element.37), channel_id=1, source_target_pairs={{0,2},{2,0},{4,6},{6,4},{8,10},{10,8},{12,14},{14,12},{16,18},{18,... | collective-permute-start | bytes 1032200 | tf_op jit(solution)/shard_map/ppermute | solution.py:32
  29.5 14.1 %collective-permute-start.10 = (bf16[2,96,896]{2,1,0:T(8,128)(2,1)S(1)}, bf16[2,96,896]{2,1,0:T(8,128)(2,1)S(1)}, u32[]{:S(2)}, u32[]{:S(2)}) collective-permute-start(bf16[2,96,896]{2,1,0:T(8,128)(2,1)S(1)} %get-tuple-element.38), channel_id=1, source_target_pairs={{0,4},{2,6},{4,0},{6,2},{8,12},{10,14},{12,8},{14,10},{16,20},{18,... | collective-permute-start | bytes 1032200 | tf_op jit(solution)/shard_map/ppermute | solution.py:32
  32.1 12.5 %collective-permute-start.11 = (bf16[2,96,896]{2,1,0:T(8,128)(2,1)S(1)}, bf16[2,96,896]{2,1,0:T(8,128)(2,1)S(1)}, u32[]{:S(2)}, u32[]{:S(2)}) collective-permute-start(bf16[2,96,896]{2,1,0:T(8,128)(2,1)S(1)} %get-tuple-element.39), channel_id=1, source_target_pairs={{0,6},{2,4},{4,2},{6,0},{8,14},{10,12},{12,10},{14,8},{16,22},{18,... | collective-permute-start | bytes 1032200 | tf_op jit(solution)/shard_map/ppermute | solution.py:32
  45.7 10.6 %collective-permute-start.19 = (bf16[2,4,96,1024]{3,2,1,0:T(8,128)(2,1)S(1)}, bf16[2,4,96,1024]{3,2,1,0:T(8,128)(2,1)S(1)}, u32[]{:S(2)}, u32[]{:S(2)}) collective-permute-start(bf16[2,4,96,1024]{3,2,1,0:T(8,128)(2,1)S(1)} %get-tuple-element.47), channel_id=1, source_target_pairs={{0,8},{2,10},{4,12},{6,14},{8,0},{10,2},{12,4},{14,6},{16,24},{18,... | collective-permute-start | bytes 4718600 | tf_op jit(solution)/shard_map/ppermute | solution.py:32
  52.3 10.5 %collective-permute-start.16 = (bf16[1,96,896]{2,1,0:T(8,128)(2,1)S(1)}, bf16[1,96,896]{2,1,0:T(8,128)(2,1)S(1)}, u32[]{:S(2)}, u32[]{:S(2)}) collective-permute-start(bf16[1,96,896]{2,1,0:T(8,128)(2,1)S(1)} %get-tuple-element.43), channel_id=1, source_target_pairs={{0,4},{2,6},{4,0},{6,2},{8,12},{10,14},{12,8},{14,10},{16,20},{18,... | collective-permute-start | bytes 516104 | tf_op jit(solution)/shard_map/ppermute | solution.py:32
  53.5 10.5 %collective-permute-start.17 = (bf16[1,96,896]{2,1,0:T(8,128)(2,1)S(1)}, bf16[1,96,896]{2,1,0:T(8,128)(2,1)S(1)}, u32[]{:S(2)}, u32[]{:S(2)}) collective-permute-start(bf16[1,96,896]{2,1,0:T(8,128)(2,1)S(1)} %get-tuple-element.44), channel_id=1, source_target_pairs={{0,6},{2,4},{4,2},{6,0},{8,14},{10,12},{12,10},{14,8},{16,22},{18,... | collective-permute-start | bytes 516104 | tf_op jit(solution)/shard_map/ppermute | solution.py:32
  58.9 14.1 %collective-permute-start.20 = (bf16[3,96,896]{2,1,0:T(8,128)(2,1)S(1)}, bf16[3,96,896]{2,1,0:T(8,128)(2,1)S(1)}, u32[]{:S(2)}, u32[]{:S(2)}) collective-permute-start(bf16[3,96,896]{2,1,0:T(8,128)(2,1)S(1)} %get-tuple-element.49), channel_id=1, source_target_pairs={{0,2},{2,0},{4,6},{6,4},{8,10},{10,8},{12,14},{14,12},{16,18},{18,... | collective-permute-start | bytes 1548296 | tf_op jit(solution)/shard_map/ppermute | solution.py:32
  59.0 24.8 %collective-permute-start.21 = (bf16[3,96,896]{2,1,0:T(8,128)(2,1)S(1)}, bf16[3,96,896]{2,1,0:T(8,128)(2,1)S(1)}, u32[]{:S(2)}, u32[]{:S(2)}) collective-permute-start(bf16[3,96,896]{2,1,0:T(8,128)(2,1)S(1)} %get-tuple-element.50), channel_id=1, source_target_pairs={{0,4},{2,6},{4,0},{6,2},{8,12},{10,14},{12,8},{14,10},{16,20},{18,... | collective-permute-start | bytes 1548296 | tf_op jit(solution)/shard_map/ppermute | solution.py:32
  60.1 25.6 %collective-permute-start.22 = (bf16[3,96,896]{2,1,0:T(8,128)(2,1)S(1)}, bf16[3,96,896]{2,1,0:T(8,128)(2,1)S(1)}, u32[]{:S(2)}, u32[]{:S(2)}) collective-permute-start(bf16[3,96,896]{2,1,0:T(8,128)(2,1)S(1)} %get-tuple-element.51), channel_id=1, source_target_pairs={{0,6},{2,4},{4,2},{6,0},{8,14},{10,12},{12,10},{14,8},{16,22},{18,... | collective-permute-start | bytes 1548296 | tf_op jit(solution)/shard_map/ppermute | solution.py:32
  64.3 27.0 %collective-permute-start.18 = (bf16[3,96,896]{2,1,0:T(8,128)(2,1)S(1)}, bf16[3,96,896]{2,1,0:T(8,128)(2,1)S(1)}, u32[]{:S(2)}, u32[]{:S(2)}) collective-permute-start(bf16[3,96,896]{2,1,0:T(8,128)(2,1)S(1)} %get-tuple-element.46.refs_4_), channel_id=1, source_target_pairs={{0,1},{2,3},{4,5},{6,7},{8,9},{10,11},{12,13},{14,15},{16,17},{18,... | collective-permute-start | bytes 1548296 | tf_op jit(solution)/shard_map/ppermute | solution.py:32
  86.0 31.7 %collective-permute-start.26 = (bf16[3,96,896]{2,1,0:T(8,128)(2,1)S(1)}, bf16[3,96,896]{2,1,0:T(8,128)(2,1)S(1)}, u32[]{:S(2)}, u32[]{:S(2)}) collective-permute-start(bf16[3,96,896]{2,1,0:T(8,128)(2,1)S(1)} %get-tuple-element.52.refs_2_), channel_id=1, source_target_pairs={{0,1},{2,3},{4,5},{6,7},{8,9},{10,11},{12,13},{14,15},{16,17},{18,... | collective-permute-start | bytes 1548296 | tf_op jit(solution)/shard_map/ppermute | solution.py:32
  91.6 17.5 %collective-permute-start.24 = (bf16[2,96,896]{2,1,0:T(8,128)(2,1)S(1)}, bf16[2,96,896]{2,1,0:T(8,128)(2,1)S(1)}, u32[]{:S(2)}, u32[]{:S(2)}) collective-permute-start(bf16[2,96,896]{2,1,0:T(8,128)(2,1)S(1)} %get-tuple-element.53.refs_0_), channel_id=1, source_target_pairs={{0,4},{2,6},{4,0},{6,2},{8,12},{10,14},{12,8},{14,10},{16,20},{18,... | collective-permute-start | bytes 1032200 | tf_op jit(solution)/shard_map/ppermute | solution.py:32
  95.5 13.6 %collective-permute-start.25 = (bf16[2,96,896]{2,1,0:T(8,128)(2,1)S(1)}, bf16[2,96,896]{2,1,0:T(8,128)(2,1)S(1)}, u32[]{:S(2)}, u32[]{:S(2)}) collective-permute-start(bf16[2,96,896]{2,1,0:T(8,128)(2,1)S(1)} %get-tuple-element.53.refs_0_), channel_id=1, source_target_pairs={{0,6},{2,4},{4,2},{6,0},{8,14},{10,12},{12,10},{14,8},{16,22},{18,... | collective-permute-start | bytes 1032200 | tf_op jit(solution)/shard_map/ppermute | solution.py:32
  118.1 18.5 %collective-permute-start.28 = (bf16[2,96,896]{2,1,0:T(8,128)(2,1)S(1)}, bf16[2,96,896]{2,1,0:T(8,128)(2,1)S(1)}, u32[]{:S(2)}, u32[]{:S(2)}) collective-permute-start(bf16[2,96,896]{2,1,0:T(8,128)(2,1)S(1)} %get-tuple-element.55.refs_0_.refs_4_), channel_id=1, source_target_pairs={{0,4},{2,6},{4,0},{6,2},{8,12},{10,14},{12,8},{14,10},{16,20},{18,... | collective-permute-start | bytes 1032200 | tf_op jit(solution)/shard_map/ppermute | solution.py:32
  121.9 16.7 %collective-permute-start.29 = (bf16[2,96,896]{2,1,0:T(8,128)(2,1)S(1)}, bf16[2,96,896]{2,1,0:T(8,128)(2,1)S(1)}, u32[]{:S(2)}, u32[]{:S(2)}) collective-permute-start(bf16[2,96,896]{2,1,0:T(8,128)(2,1)S(1)} %get-tuple-element.55.refs_0_.refs_4_), channel_id=1, source_target_pairs={{0,6},{2,4},{4,2},{6,0},{8,14},{10,12},{12,10},{14,8},{16,22},{18,... | collective-permute-start | bytes 1032200 | tf_op jit(solution)/shard_map/ppermute | solution.py:32
  140.5 10.9 %collective-permute-start.30 = (f32[4,96,1024]{2,1,0:T(8,128)S(1)}, f32[4,96,1024]{2,1,0:T(8,128)S(1)}, u32[]{:S(2)}, u32[]{:S(2)}) collective-permute-start(f32[4,96,1024]{2,1,0:T(8,128)S(1)} %shard_map.95), channel_id=1, source_target_pairs={{0,8},{2,10},{4,12},{6,14},{8,0},{10,2},{12,4},{14,6},{16,24},{18,... | collective-permute-start | bytes 4718600 | tf_op jit(solution)/shard_map/ppermute | solution.py:32
  145.4 16.8 %collective-permute-start.35 = (bf16[2,96,896]{2,1,0:T(8,128)(2,1)S(1)}, bf16[2,96,896]{2,1,0:T(8,128)(2,1)S(1)}, u32[]{:S(2)}, u32[]{:S(2)}) collective-permute-start(bf16[2,96,896]{2,1,0:T(8,128)(2,1)S(1)} %shard_map.98.refs_0_), channel_id=1, source_target_pairs={{0,4},{2,6},{4,0},{6,2},{8,12},{10,14},{12,8},{14,10},{16,20},{18,... | collective-permute-start | bytes 1032200 | tf_op jit(solution)/shard_map/ppermute | solution.py:32
  146.6 17.6 %collective-permute-start.36 = (bf16[2,96,896]{2,1,0:T(8,128)(2,1)S(1)}, bf16[2,96,896]{2,1,0:T(8,128)(2,1)S(1)}, u32[]{:S(2)}, u32[]{:S(2)}) collective-permute-start(bf16[2,96,896]{2,1,0:T(8,128)(2,1)S(1)} %shard_map.98.refs_0_), channel_id=1, source_target_pairs={{0,6},{2,4},{4,2},{6,0},{8,14},{10,12},{12,10},{14,8},{16,22},{18,... | collective-permute-start | bytes 1032200 | tf_op jit(solution)/shard_map/ppermute | solution.py:32
  152.5 11.8 %collective-permute-start.31 = (bf16[96,1024]{1,0:T(8,128)(2,1)S(1)}, bf16[96,1024]{1,0:T(8,128)(2,1)S(1)}, u32[]{:S(2)}, u32[]{:S(2)}) collective-permute-start(bf16[96,1024]{1,0:T(8,128)(2,1)S(1)} %get-tuple-element.57), channel_id=1, source_target_pairs={{0,16},{2,18},{4,20},{6,22},{8,24},{10,26},{12,28},{14,30},{16,0},... | collective-permute-start | bytes 589832 | tf_op jit(solution)/shard_map/ppermute | solution.py:32
  152.5 11.8 %collective-permute-start.32 = (bf16[96,1024]{1,0:T(8,128)(2,1)S(1)}, bf16[96,1024]{1,0:T(8,128)(2,1)S(1)}, u32[]{:S(2)}, u32[]{:S(2)}) collective-permute-start(bf16[96,1024]{1,0:T(8,128)(2,1)S(1)} %get-tuple-element.58), channel_id=1, source_target_pairs={{0,32},{2,34},{4,36},{6,38},{8,40},{10,42},{12,44},{14,46},{16,48}... | collective-permute-start | bytes 589832 | tf_op jit(solution)/shard_map/ppermute | solution.py:32
  155.1 10.0 %collective-permute-start.33 = (bf16[96,1024]{1,0:T(8,128)(2,1)S(1)}, bf16[96,1024]{1,0:T(8,128)(2,1)S(1)}, u32[]{:S(2)}, u32[]{:S(2)}) collective-permute-start(bf16[96,1024]{1,0:T(8,128)(2,1)S(1)} %get-tuple-element.59), channel_id=1, source_target_pairs={{0,48},{2,50},{4,52},{6,54},{8,56},{10,58},{12,60},{14,62},{16,32}... | collective-permute-start | bytes 589832 | tf_op jit(solution)/shard_map/ppermute | solution.py:32
  (26 other events, 174.6 us)

commit v3 on v2

--- a/solution.py
+++ b/solution.py
@@ -189,20 +189,32 @@
     out[...] = (own[...] + p1[...] + p2[...] + p3[...]).astype(BF16)
 
 
-def reduce_tokens(y, mine, theirs, later_than):
+def join_step(y, mine, theirs):
     outs = [shape(ROWS, WIDE, dtype=F32)] + [shape(ROWS, WIDE)] * 3
-    total, *parts = call(join_kernel, [mine, theirs], outs, 12, (), y)
+    return call(join_kernel, [mine, theirs], outs, 12, (), y)
+
+
+def sum_step(total, parts, later_than):
     got = [swap_x(part, j + 1) for j, part in enumerate(parts)]
-    sums = call(sum_kernel, [total, *got], [shape(PART, WIDE, dtype=F32)] * 4, 8, later_than)
-    got = [swap_z(part, j + 1) for j, part in enumerate(sums[1:])]
-    return call(add_kernel, [sums[0], *got], [shape(PART, WIDE)], 4)[0]
-
-
-def rows_kernel(*refs):
-    blocks, outs = refs[:8], refs[8:]
+    return call(sum_kernel, [total, *got], [shape(PART, WIDE, dtype=F32)] * 4, 8, later_than)
+
+
+def rows_kernel(index, *refs):
+    blocks, out = refs[:8], refs[8]
+    for k, block in enumerate(blocks):
+        out[k * ROWS : (k + 1) * ROWS] = block[index]
+
+
+def rows_step(index, blocks, flops=1, later_than=()):
+    kernel = functools.partial(rows_kernel, index)
+    return call(kernel, blocks, [shape(8 * ROWS, HID)], 16, later_than, flops=flops)[0]
+
+
+def tokens_kernel(first, second, *outs):
     for i, out in enumerate(outs):
-        for k, block in enumerate(blocks):
-            out[k * ROWS : (k + 1) * ROWS] = block[i]
+        for k in range(4):
+            out[k * ROWS : (k + 1) * ROWS] = first[i, k]
+            out[(k + 4) * ROWS : (k + 5) * ROWS] = second[i, k]
 
 
 def hidden_rows_kernel(*refs):
@@ -256,16 +268,17 @@
     (hidden,) = call(stack_kernel, [hidden1, hidden2], [shape(2, ROWS, HID)], 4, blocks2[1:])
     hiddens = [hidden] + swap_all_y([hidden] * 3)
 
-    rows = [shape(8 * ROWS, HID)]
-    gate_grad, up_grad = call(rows_kernel, [*blocks1, *blocks2], rows * 2, 16)
-    (hidden,) = call(hidden_rows_kernel, hiddens, rows, 12)
-    xs, gs = (
-        jnp.concatenate([t[i].reshape(4 * ROWS, WIDE) for t in (tokens1, tokens2)], axis=0)
-        for i in range(2)
-    )
-    grad_gate, grad_up = dot(xs, gate_grad), dot(xs, up_grad)
-    before = [grad_gate[:16, :128], grad_up[:16, :128], *hiddens[1:]]
-    grad_in = reduce_tokens(y, mine, theirs, before)
+    blocks = [*blocks1, *blocks2]
+    gate_grad = rows_step(0, blocks, 2 * 8 * ROWS * WIDE * HID)
+    total, *parts = join_step(y, mine, theirs)
+    outs = [shape(8 * ROWS, WIDE)] * 2
+    xs, gs = call(tokens_kernel, [tokens1, tokens2], outs, 16, parts[:1])
+    grad_gate = dot(xs, gate_grad)
+    sums = sum_step(total, parts, [grad_gate[:16, :128], *hiddens[1:]])
+    grad_up = dot(xs, rows_step(1, blocks, 1, sums[:1]))
+    (hidden,) = call(hidden_rows_kernel, hiddens, [shape(8 * ROWS, HID)], 12, sums[:1])
+    got = [swap_z(part, j + 1) for j, part in enumerate(sums[1:])]
+    (grad_in,) = call(add_kernel, [sums[0], *got], [shape(PART, WIDE)], 4)
     return grad_in, grad_gate, grad_up, dot(hidden, gs)
 
 

time: 177 us -> 175 us (0.989); the launches traced: 175 us -> 174 us
    unnamed x20 -> x18, local copies, waits for them, and re-layouts: 5.57 us -> 4.52 us
    pallas_call x18 -> x20, Pallas kernels: 11.5 us -> 11.8 us  [call(): pl.pallas_call(run, out_shape=outs, in_specs=[SMEM] * first + [VMEM] * (l...]
  transfers between devices with their start and end apart: 40 -> 40, of which waited for: 24 -> 21; matrix products, arithmetic and copies ran while one was open for 4% -> 4% of each run, Pallas kernels for 4% -> 5%
where the time goes in v3:
time: 175 us; the launch traced here: 174 us
  waiting for transfers between devices  84.7 us (48%)
  starting transfers between devices  64.7 us (37%)
  Pallas kernels  11.8 us (7%)
  matrix products  7.8 us (4%)
  local copies, waits for them, and re-layouts  4.53 us (3%)
    ppermute x40, waiting for transfers between devices, swap(): return lax.ppermute(value, AXES, pairs)  84.7 us
    ppermute x40, starting transfers between devices, swap(): return lax.ppermute(value, AXES, pairs)  64.7 us
    pallas_call x20, Pallas kernels, call(): pl.pallas_call(run, out_shape=outs, in_specs=[SMEM] * first + [VMEM] * (l...  11.8 us
    dot_general x3, matrix products, dot(): lax.dot_general(left, right, (((0,), (0,)), ((), ())), preferred_element_...  7.8 us
    unnamed x18, local copies, waits for them, and re-layouts  4.52 us
  transfers between devices with their start and end apart: 40, of which 21 were waited for; matrix products, arithmetic and copies ran while one was open for 4% of the time, Pallas kernels for 5%

profile of v3, /device:TPU:1, one launch (start us, length us, event | category | flops | bytes accessed | tf_op | source)
XLA Modules:
  0.0 174.5 jit_solution(9779206472133791524)
XLA Ops:
  3.2 3.0 %collective-permute-start.1 = (bf16[24,1024]{1,0:T(8,128)(2,1)}, bf16[24,1024]{1,0:T(8,128)(2,1)S(1)}, u32[]{:S(2)}, u32[]{:S(2)}) collective-permute-start(bf16[24,1024]{1,0:T(8,128)(2,1)} %refs_0_.4), channel_id=1, source_target_pairs={{0,128},{2,130},{4,132},{6,134},{8,136},{10,138},{12,140},{14,142}... | collective-permute-start | bytes 147464 | tf_op jit(solution)/shard_map/ppermute | solution.py:32
  20.4 2.9 %collective-permute-done.8.refs_3_ = bf16[24,1024]{1,0:T(8,128)(2,1)S(1)} collective-permute-done((bf16[24,1024]{1,0:T(8,128)(2,1)S(1)}, bf16[24,1024]{1,0:T(8,128)(2,1)S(1)}, u32[]{:S(2)}, u32[]{:S(2)}) %collective-permute-start.8) | collective-permute-done | bytes 49184 | tf_op jit(solution)/shard_map/ppermute | solution.py:32
  34.7 3.4 %collective-permute-done.13.refs_3_ = bf16[96,1024]{1,0:T(8,128)(2,1)S(1)} collective-permute-done((bf16[96,1024]{1,0:T(8,128)(2,1)S(1)}, bf16[96,1024]{1,0:T(8,128)(2,1)S(1)}, u32[]{:S(2)}, u32[]{:S(2)}) %collective-permute-start.13) | collective-permute-done | bytes 196640 | tf_op jit(solution)/shard_map/ppermute | solution.py:32
  40.2 3.4 %collective-permute-done.10.refs_8_.refs_2_ = bf16[2,96,896]{2,1,0:T(8,128)(2,1)S(1)} collective-permute-done((bf16[2,96,896]{2,1,0:T(8,128)(2,1)S(1)}, bf16[2,96,896]{2,1,0:T(8,128)(2,1)S(1)}, u32[]{:S(2)}, u32[]{:S(2)}) %collective-permute-start.10) | collective-permute-done | bytes 344096 | tf_op jit(solution)/shard_map/ppermute | solution.py:32
  45.7 6.7 %collective-permute-start.19 = (bf16[2,4,96,1024]{3,2,1,0:T(8,128)(2,1)S(1)}, bf16[2,4,96,1024]{3,2,1,0:T(8,128)(2,1)S(1)}, u32[]{:S(2)}, u32[]{:S(2)}) collective-permute-start(bf16[2,4,96,1024]{3,2,1,0:T(8,128)(2,1)S(1)} %get-tuple-element.47.refs_0_), channel_id=1, source_target_pairs={{0,8},{2,10},{4,12},{6,14},{8,0},{10,2},{12,4},{14,6},{16,24},{18,... | collective-permute-start | bytes 4718600 | tf_op jit(solution)/shard_map/ppermute | solution.py:32
  53.5 2.7 %collective-permute-start.17 = (bf16[1,96,896]{2,1,0:T(8,128)(2,1)S(1)}, bf16[1,96,896]{2,1,0:T(8,128)(2,1)S(1)}, u32[]{:S(2)}, u32[]{:S(2)}) collective-permute-start(bf16[1,96,896]{2,1,0:T(8,128)(2,1)S(1)} %get-tuple-element.44), channel_id=1, source_target_pairs={{0,6},{2,4},{4,2},{6,0},{8,14},{10,12},{12,10},{14,8},{16,22},{18,... | collective-permute-start | bytes 516104 | tf_op jit(solution)/shard_map/ppermute | solution.py:32
  64.3 5.3 %collective-permute-start.18 = (bf16[3,96,896]{2,1,0:T(8,128)(2,1)S(1)}, bf16[3,96,896]{2,1,0:T(8,128)(2,1)S(1)}, u32[]{:S(2)}, u32[]{:S(2)}) collective-permute-start(bf16[3,96,896]{2,1,0:T(8,128)(2,1)S(1)} %get-tuple-element.46.refs_4_), channel_id=1, source_target_pairs={{0,1},{2,3},{4,5},{6,7},{8,9},{10,11},{12,13},{14,15},{16,17},{18,... | collective-permute-start | bytes 1548296 | tf_op jit(solution)/shard_map/ppermute | solution.py:32
  69.5 3.4 %collective-permute-done.20.refs_1_ = bf16[3,96,896]{2,1,0:T(8,128)(2,1)S(1)} collective-permute-done((bf16[3,96,896]{2,1,0:T(8,128)(2,1)S(1)}, bf16[3,96,896]{2,1,0:T(8,128)(2,1)S(1)}, u32[]{:S(2)}, u32[]{:S(2)}) %collective-permute-start.20) | collective-permute-done | bytes 516128 | tf_op jit(solution)/shard_map/ppermute | solution.py:32
  72.9 10.8 %collective-permute-done.21.refs_2_ = bf16[3,96,896]{2,1,0:T(8,128)(2,1)S(1)} collective-permute-done((bf16[3,96,896]{2,1,0:T(8,128)(2,1)S(1)}, bf16[3,96,896]{2,1,0:T(8,128)(2,1)S(1)}, u32[]{:S(2)}, u32[]{:S(2)}) %collective-permute-start.21) | collective-permute-done | bytes 516128 | tf_op jit(solution)/shard_map/ppermute | solution.py:32
  86.0 5.3 %collective-permute-start.26 = (bf16[3,96,896]{2,1,0:T(8,128)(2,1)S(1)}, bf16[3,96,896]{2,1,0:T(8,128)(2,1)S(1)}, u32[]{:S(2)}, u32[]{:S(2)}) collective-permute-start(bf16[3,96,896]{2,1,0:T(8,128)(2,1)S(1)} %get-tuple-element.52.refs_2_), channel_id=1, source_target_pairs={{0,1},{2,3},{4,5},{6,7},{8,9},{10,11},{12,13},{14,15},{16,17},{18,... | collective-permute-start | bytes 1548296 | tf_op jit(solution)/shard_map/ppermute | solution.py:32
  91.6 3.8 %collective-permute-start.24 = (bf16[2,96,896]{2,1,0:T(8,128)(2,1)S(1)}, bf16[2,96,896]{2,1,0:T(8,128)(2,1)S(1)}, u32[]{:S(2)}, u32[]{:S(2)}) collective-permute-start(bf16[2,96,896]{2,1,0:T(8,128)(2,1)S(1)} %get-tuple-element.53.refs_0_), channel_id=1, source_target_pairs={{0,4},{2,6},{4,0},{6,2},{8,12},{10,14},{12,8},{14,10},{16,20},{18,... | collective-permute-start | bytes 1032200 | tf_op jit(solution)/shard_map/ppermute | solution.py:32
  95.5 3.8 %collective-permute-done.23.refs_1_.refs_2_ = bf16[2,96,896]{2,1,0:T(8,128)(2,1)S(1)} collective-permute-done((bf16[2,96,896]{2,1,0:T(8,128)(2,1)S(1)}, bf16[2,96,896]{2,1,0:T(8,128)(2,1)S(1)}, u32[]{:S(2)}, u32[]{:S(2)}) %collective-permute-start.23) | collective-permute-done | bytes 344096 | tf_op jit(solution)/shard_map/ppermute | solution.py:32
  99.3 9.8 %collective-permute-done.24.refs_2_.refs_3_ = bf16[2,96,896]{2,1,0:T(8,128)(2,1)S(1)} collective-permute-done((bf16[2,96,896]{2,1,0:T(8,128)(2,1)S(1)}, bf16[2,96,896]{2,1,0:T(8,128)(2,1)S(1)}, u32[]{:S(2)}, u32[]{:S(2)}) %collective-permute-start.24) | collective-permute-done | bytes 344096 | tf_op jit(solution)/shard_map/ppermute | solution.py:32
  109.1 8.6 %collective-permute-done.26.refs_1_ = bf16[3,96,896]{2,1,0:T(8,128)(2,1)S(1)} collective-permute-done((bf16[3,96,896]{2,1,0:T(8,128)(2,1)S(1)}, bf16[3,96,896]{2,1,0:T(8,128)(2,1)S(1)}, u32[]{:S(2)}, u32[]{:S(2)}) %collective-permute-start.26) | collective-permute-done | bytes 516128 | tf_op jit(solution)/shard_map/ppermute | solution.py:32
  118.1 3.8 %collective-permute-start.28 = (bf16[2,96,896]{2,1,0:T(8,128)(2,1)S(1)}, bf16[2,96,896]{2,1,0:T(8,128)(2,1)S(1)}, u32[]{:S(2)}, u32[]{:S(2)}) collective-permute-start(bf16[2,96,896]{2,1,0:T(8,128)(2,1)S(1)} %get-tuple-element.55.refs_0_.refs_4_), channel_id=1, source_target_pairs={{0,4},{2,6},{4,0},{6,2},{8,12},{10,14},{12,8},{14,10},{16,20},{18,... | collective-permute-start | bytes 1032200 | tf_op jit(solution)/shard_map/ppermute | solution.py:32
  121.9 4.9 %collective-permute-done.27.refs_1_.refs_5_.refs_2_ = bf16[2,96,896]{2,1,0:T(8,128)(2,1)S(1)} collective-permute-done((bf16[2,96,896]{2,1,0:T(8,128)(2,1)S(1)}, bf16[2,96,896]{2,1,0:T(8,128)(2,1)S(1)}, u32[]{:S(2)}, u32[]{:S(2)}) %collective-permute-start.27) | collective-permute-done | bytes 344096 | tf_op jit(solution)/shard_map/ppermute | solution.py:32
  126.8 9.8 %collective-permute-done.28.refs_2_.refs_6_.refs_3_ = bf16[2,96,896]{2,1,0:T(8,128)(2,1)S(1)} collective-permute-done((bf16[2,96,896]{2,1,0:T(8,128)(2,1)S(1)}, bf16[2,96,896]{2,1,0:T(8,128)(2,1)S(1)}, u32[]{:S(2)}, u32[]{:S(2)}) %collective-permute-start.28) | collective-permute-done | bytes 344096 | tf_op jit(solution)/shard_map/ppermute | solution.py:32
  146.3 2.7 %collective-permute-start.36 = (bf16[2,96,896]{2,1,0:T(8,128)(2,1)S(1)}, bf16[2,96,896]{2,1,0:T(8,128)(2,1)S(1)}, u32[]{:S(2)}, u32[]{:S(2)}) collective-permute-start(bf16[2,96,896]{2,1,0:T(8,128)(2,1)S(1)} %shard_map.99.refs_0_), channel_id=1, source_target_pairs={{0,6},{2,4},{4,2},{6,0},{8,14},{10,12},{12,10},{14,8},{16,22},{18,... | collective-permute-start | bytes 1032200 | tf_op jit(solution)/shard_map/ppermute | solution.py:32
  149.8 3.1 %collective-permute-done.34.refs_5_.refs_1_ = bf16[2,96,896]{2,1,0:T(8,128)(2,1)S(1)} collective-permute-done((bf16[2,96,896]{2,1,0:T(8,128)(2,1)S(1)}, bf16[2,96,896]{2,1,0:T(8,128)(2,1)S(1)}, u32[]{:S(2)}, u32[]{:S(2)}) %collective-permute-start.34) | collective-permute-done | bytes 344096 | tf_op jit(solution)/shard_map/ppermute | solution.py:32
  155.5 4.5 %collective-permute-done.35.refs_6_.refs_2_ = bf16[2,96,896]{2,1,0:T(8,128)(2,1)S(1)} collective-permute-done((bf16[2,96,896]{2,1,0:T(8,128)(2,1)S(1)}, bf16[2,96,896]{2,1,0:T(8,128)(2,1)S(1)}, u32[]{:S(2)}, u32[]{:S(2)}) %collective-permute-start.35) | collective-permute-done | bytes 344096 | tf_op jit(solution)/shard_map/ppermute | solution.py:32
  160.0 3.9 %collective-permute-done.36.refs_7_.refs_3_ = bf16[2,96,896]{2,1,0:T(8,128)(2,1)S(1)} collective-permute-done((bf16[2,96,896]{2,1,0:T(8,128)(2,1)S(1)}, bf16[2,96,896]{2,1,0:T(8,128)(2,1)S(1)}, u32[]{:S(2)}, u32[]{:S(2)}) %collective-permute-start.36) | collective-permute-done | bytes 344096 | tf_op jit(solution)/shard_map/ppermute | solution.py:32
  164.2 3.4 %collective-permute-start.39 = (f32[24,1024]{1,0:T(8,128)S(1)}, f32[24,1024]{1,0:T(8,128)S(1)}, u32[]{:S(2)}, u32[]{:S(2)}) collective-permute-start(f32[24,1024]{1,0:T(8,128)S(1)} %get-tuple-element.66), channel_id=1, source_target_pairs={{0,192},{2,194},{4,196},{6,198},{8,200},{10,202},{12,204},{14,206}... | collective-permute-start | bytes 294920 | tf_op jit(solution)/shard_map/ppermute | solution.py:32
  167.8 3.1 %convolution_convert_fusion.1 = bf16[1024,896]{1,0:T(8,128)(2,1)} fusion(bf16[768,1024]{1,0:T(8,128)(2,1)S(1)} %get-tuple-element.60, bf16[768,896]{1,0:T(8,128)(2,1)S(1)} %shard_map.102), kind=kOutput, calls=%fused_computation.1 | convolution fusion | flops 1410203648 | bytes 4784128 | tf_op jit(solution)/shard_map/dot_general | solution.py:234
  171.0 2.9 %convolution_convert_fusion = bf16[896,1024]{1,0:T(8,128)(2,1)} fusion(bf16[768,896]{1,0:T(8,128)(2,1)S(1)} %shard_map.103, bf16[768,1024]{1,0:T(8,128)(2,1)S(1)} %get-tuple-element.67), kind=kOutput, calls=%fused_computation | convolution fusion | flops 1410203648 | bytes 4784128 | tf_op jit(solution)/shard_map/dot_general | solution.py:234
  (98 shorter events, 58.6 us)
Async XLA Ops:
  11.2 12.4 %collective-permute-start.3 = (bf16[96,1024]{1,0:T(8,128)(2,1)S(1)}, bf16[96,1024]{1,0:T(8,128)(2,1)S(1)}, u32[]{:S(2)}, u32[]{:S(2)}) collective-permute-start(bf16[96,1024]{1,0:T(8,128)(2,1)S(1)} %shard_map.85.refs_1_), channel_id=1, source_target_pairs={{0,16},{2,18},{4,20},{6,22},{8,24},{10,26},{12,28},{14,30},{16,0},... | collective-permute-start | bytes 589832 | tf_op jit(solution)/shard_map/ppermute | solution.py:32
  12.5 11.1 %collective-permute-start.4 = (bf16[96,1024]{1,0:T(8,128)(2,1)S(1)}, bf16[96,1024]{1,0:T(8,128)(2,1)S(1)}, u32[]{:S(2)}, u32[]{:S(2)}) collective-permute-start(bf16[96,1024]{1,0:T(8,128)(2,1)S(1)} %shard_map.85.refs_1_), channel_id=1, source_target_pairs={{0,32},{2,34},{4,36},{6,38},{8,40},{10,42},{12,44},{14,46},{16,48}... | collective-permute-start | bytes 589832 | tf_op jit(solution)/shard_map/ppermute | solution.py:32
  23.4 10.9 %collective-permute-start.12 = (bf16[96,1024]{1,0:T(8,128)(2,1)S(1)}, bf16[96,1024]{1,0:T(8,128)(2,1)S(1)}, u32[]{:S(2)}, u32[]{:S(2)}) collective-permute-start(bf16[96,1024]{1,0:T(8,128)(2,1)S(1)} %shard_map.86.refs_7_.refs_1_), channel_id=1, source_target_pairs={{0,16},{2,18},{4,20},{6,22},{8,24},{10,26},{12,28},{14,30},{16,0},... | collective-permute-start | bytes 589832 | tf_op jit(solution)/shard_map/ppermute | solution.py:32
  28.1 12.1 %collective-permute-start.9 = (bf16[2,96,896]{2,1,0:T(8,128)(2,1)S(1)}, bf16[2,96,896]{2,1,0:T(8,128)(2,1)S(1)}, u32[]{:S(2)}, u32[]{:S(2)}) collective-permute-start(bf16[2,96,896]{2,1,0:T(8,128)(2,1)S(1)} %get-tuple-element.37), channel_id=1, source_target_pairs={{0,2},{2,0},{4,6},{6,4},{8,10},{10,8},{12,14},{14,12},{16,18},{18,... | collective-permute-start | bytes 1032200 | tf_op jit(solution)/shard_map/ppermute | solution.py:32
  29.5 14.1 %collective-permute-start.10 = (bf16[2,96,896]{2,1,0:T(8,128)(2,1)S(1)}, bf16[2,96,896]{2,1,0:T(8,128)(2,1)S(1)}, u32[]{:S(2)}, u32[]{:S(2)}) collective-permute-start(bf16[2,96,896]{2,1,0:T(8,128)(2,1)S(1)} %get-tuple-element.38), channel_id=1, source_target_pairs={{0,4},{2,6},{4,0},{6,2},{8,12},{10,14},{12,8},{14,10},{16,20},{18,... | collective-permute-start | bytes 1032200 | tf_op jit(solution)/shard_map/ppermute | solution.py:32
  32.1 12.5 %collective-permute-start.11 = (bf16[2,96,896]{2,1,0:T(8,128)(2,1)S(1)}, bf16[2,96,896]{2,1,0:T(8,128)(2,1)S(1)}, u32[]{:S(2)}, u32[]{:S(2)}) collective-permute-start(bf16[2,96,896]{2,1,0:T(8,128)(2,1)S(1)} %get-tuple-element.39), channel_id=1, source_target_pairs={{0,6},{2,4},{4,2},{6,0},{8,14},{10,12},{12,10},{14,8},{16,22},{18,... | collective-permute-start | bytes 1032200 | tf_op jit(solution)/shard_map/ppermute | solution.py:32
  45.7 10.6 %collective-permute-start.19 = (bf16[2,4,96,1024]{3,2,1,0:T(8,128)(2,1)S(1)}, bf16[2,4,96,1024]{3,2,1,0:T(8,128)(2,1)S(1)}, u32[]{:S(2)}, u32[]{:S(2)}) collective-permute-start(bf16[2,4,96,1024]{3,2,1,0:T(8,128)(2,1)S(1)} %get-tuple-element.47.refs_0_), channel_id=1, source_target_pairs={{0,8},{2,10},{4,12},{6,14},{8,0},{10,2},{12,4},{14,6},{16,24},{18,... | collective-permute-start | bytes 4718600 | tf_op jit(solution)/shard_map/ppermute | solution.py:32
  52.3 10.5 %collective-permute-start.16 = (bf16[1,96,896]{2,1,0:T(8,128)(2,1)S(1)}, bf16[1,96,896]{2,1,0:T(8,128)(2,1)S(1)}, u32[]{:S(2)}, u32[]{:S(2)}) collective-permute-start(bf16[1,96,896]{2,1,0:T(8,128)(2,1)S(1)} %get-tuple-element.43), channel_id=1, source_target_pairs={{0,4},{2,6},{4,0},{6,2},{8,12},{10,14},{12,8},{14,10},{16,20},{18,... | collective-permute-start | bytes 516104 | tf_op jit(solution)/shard_map/ppermute | solution.py:32
  53.5 10.5 %collective-permute-start.17 = (bf16[1,96,896]{2,1,0:T(8,128)(2,1)S(1)}, bf16[1,96,896]{2,1,0:T(8,128)(2,1)S(1)}, u32[]{:S(2)}, u32[]{:S(2)}) collective-permute-start(bf16[1,96,896]{2,1,0:T(8,128)(2,1)S(1)} %get-tuple-element.44), channel_id=1, source_target_pairs={{0,6},{2,4},{4,2},{6,0},{8,14},{10,12},{12,10},{14,8},{16,22},{18,... | collective-permute-start | bytes 516104 | tf_op jit(solution)/shard_map/ppermute | solution.py:32
  58.9 14.1 %collective-permute-start.20 = (bf16[3,96,896]{2,1,0:T(8,128)(2,1)S(1)}, bf16[3,96,896]{2,1,0:T(8,128)(2,1)S(1)}, u32[]{:S(2)}, u32[]{:S(2)}) collective-permute-start(bf16[3,96,896]{2,1,0:T(8,128)(2,1)S(1)} %get-tuple-element.49), channel_id=1, source_target_pairs={{0,2},{2,0},{4,6},{6,4},{8,10},{10,8},{12,14},{14,12},{16,18},{18,... | collective-permute-start | bytes 1548296 | tf_op jit(solution)/shard_map/ppermute | solution.py:32
  59.0 24.8 %collective-permute-start.21 = (bf16[3,96,896]{2,1,0:T(8,128)(2,1)S(1)}, bf16[3,96,896]{2,1,0:T(8,128)(2,1)S(1)}, u32[]{:S(2)}, u32[]{:S(2)}) collective-permute-start(bf16[3,96,896]{2,1,0:T(8,128)(2,1)S(1)} %get-tuple-element.50), channel_id=1, source_target_pairs={{0,4},{2,6},{4,0},{6,2},{8,12},{10,14},{12,8},{14,10},{16,20},{18,... | collective-permute-start | bytes 1548296 | tf_op jit(solution)/shard_map/ppermute | solution.py:32
  60.1 25.6 %collective-permute-start.22 = (bf16[3,96,896]{2,1,0:T(8,128)(2,1)S(1)}, bf16[3,96,896]{2,1,0:T(8,128)(2,1)S(1)}, u32[]{:S(2)}, u32[]{:S(2)}) collective-permute-start(bf16[3,96,896]{2,1,0:T(8,128)(2,1)S(1)} %get-tuple-element.51), channel_id=1, source_target_pairs={{0,6},{2,4},{4,2},{6,0},{8,14},{10,12},{12,10},{14,8},{16,22},{18,... | collective-permute-start | bytes 1548296 | tf_op jit(solution)/shard_map/ppermute | solution.py:32
  64.3 27.0 %collective-permute-start.18 = (bf16[3,96,896]{2,1,0:T(8,128)(2,1)S(1)}, bf16[3,96,896]{2,1,0:T(8,128)(2,1)S(1)}, u32[]{:S(2)}, u32[]{:S(2)}) collective-permute-start(bf16[3,96,896]{2,1,0:T(8,128)(2,1)S(1)} %get-tuple-element.46.refs_4_), channel_id=1, source_target_pairs={{0,1},{2,3},{4,5},{6,7},{8,9},{10,11},{12,13},{14,15},{16,17},{18,... | collective-permute-start | bytes 1548296 | tf_op jit(solution)/shard_map/ppermute | solution.py:32
  86.0 31.7 %collective-permute-start.26 = (bf16[3,96,896]{2,1,0:T(8,128)(2,1)S(1)}, bf16[3,96,896]{2,1,0:T(8,128)(2,1)S(1)}, u32[]{:S(2)}, u32[]{:S(2)}) collective-permute-start(bf16[3,96,896]{2,1,0:T(8,128)(2,1)S(1)} %get-tuple-element.52.refs_2_), channel_id=1, source_target_pairs={{0,1},{2,3},{4,5},{6,7},{8,9},{10,11},{12,13},{14,15},{16,17},{18,... | collective-permute-start | bytes 1548296 | tf_op jit(solution)/shard_map/ppermute | solution.py:32
  91.6 17.5 %collective-permute-start.24 = (bf16[2,96,896]{2,1,0:T(8,128)(2,1)S(1)}, bf16[2,96,896]{2,1,0:T(8,128)(2,1)S(1)}, u32[]{:S(2)}, u32[]{:S(2)}) collective-permute-start(bf16[2,96,896]{2,1,0:T(8,128)(2,1)S(1)} %get-tuple-element.53.refs_0_), channel_id=1, source_target_pairs={{0,4},{2,6},{4,0},{6,2},{8,12},{10,14},{12,8},{14,10},{16,20},{18,... | collective-permute-start | bytes 1032200 | tf_op jit(solution)/shard_map/ppermute | solution.py:32
  95.5 13.6 %collective-permute-start.25 = (bf16[2,96,896]{2,1,0:T(8,128)(2,1)S(1)}, bf16[2,96,896]{2,1,0:T(8,128)(2,1)S(1)}, u32[]{:S(2)}, u32[]{:S(2)}) collective-permute-start(bf16[2,96,896]{2,1,0:T(8,128)(2,1)S(1)} %get-tuple-element.53.refs_0_), channel_id=1, source_target_pairs={{0,6},{2,4},{4,2},{6,0},{8,14},{10,12},{12,10},{14,8},{16,22},{18,... | collective-permute-start | bytes 1032200 | tf_op jit(solution)/shard_map/ppermute | solution.py:32
  118.1 18.5 %collective-permute-start.28 = (bf16[2,96,896]{2,1,0:T(8,128)(2,1)S(1)}, bf16[2,96,896]{2,1,0:T(8,128)(2,1)S(1)}, u32[]{:S(2)}, u32[]{:S(2)}) collective-permute-start(bf16[2,96,896]{2,1,0:T(8,128)(2,1)S(1)} %get-tuple-element.55.refs_0_.refs_4_), channel_id=1, source_target_pairs={{0,4},{2,6},{4,0},{6,2},{8,12},{10,14},{12,8},{14,10},{16,20},{18,... | collective-permute-start | bytes 1032200 | tf_op jit(solution)/shard_map/ppermute | solution.py:32
  121.9 16.7 %collective-permute-start.29 = (bf16[2,96,896]{2,1,0:T(8,128)(2,1)S(1)}, bf16[2,96,896]{2,1,0:T(8,128)(2,1)S(1)}, u32[]{:S(2)}, u32[]{:S(2)}) collective-permute-start(bf16[2,96,896]{2,1,0:T(8,128)(2,1)S(1)} %get-tuple-element.55.refs_0_.refs_4_), channel_id=1, source_target_pairs={{0,6},{2,4},{4,2},{6,0},{8,14},{10,12},{12,10},{14,8},{16,22},{18,... | collective-permute-start | bytes 1032200 | tf_op jit(solution)/shard_map/ppermute | solution.py:32
  142.9 10.0 %collective-permute-start.34 = (bf16[2,96,896]{2,1,0:T(8,128)(2,1)S(1)}, bf16[2,96,896]{2,1,0:T(8,128)(2,1)S(1)}, u32[]{:S(2)}, u32[]{:S(2)}) collective-permute-start(bf16[2,96,896]{2,1,0:T(8,128)(2,1)S(1)} %shard_map.99.refs_0_), channel_id=1, source_target_pairs={{0,2},{2,0},{4,6},{6,4},{8,10},{10,8},{12,14},{14,12},{16,18},{18,... | collective-permute-start | bytes 1032200 | tf_op jit(solution)/shard_map/ppermute | solution.py:32
  145.0 15.0 %collective-permute-start.35 = (bf16[2,96,896]{2,1,0:T(8,128)(2,1)S(1)}, bf16[2,96,896]{2,1,0:T(8,128)(2,1)S(1)}, u32[]{:S(2)}, u32[]{:S(2)}) collective-permute-start(bf16[2,96,896]{2,1,0:T(8,128)(2,1)S(1)} %shard_map.99.refs_0_), channel_id=1, source_target_pairs={{0,4},{2,6},{4,0},{6,2},{8,12},{10,14},{12,8},{14,10},{16,20},{18,... | collective-permute-start | bytes 1032200 | tf_op jit(solution)/shard_map/ppermute | solution.py:32
  146.3 17.6 %collective-permute-start.36 = (bf16[2,96,896]{2,1,0:T(8,128)(2,1)S(1)}, bf16[2,96,896]{2,1,0:T(8,128)(2,1)S(1)}, u32[]{:S(2)}, u32[]{:S(2)}) collective-permute-start(bf16[2,96,896]{2,1,0:T(8,128)(2,1)S(1)} %shard_map.99.refs_0_), channel_id=1, source_target_pairs={{0,6},{2,4},{4,2},{6,0},{8,14},{10,12},{12,10},{14,8},{16,22},{18,... | collective-permute-start | bytes 1032200 | tf_op jit(solution)/shard_map/ppermute | solution.py:32
  149.3 14.6 %collective-permute-start.31 = (bf16[96,1024]{1,0:T(8,128)(2,1)S(1)}, bf16[96,1024]{1,0:T(8,128)(2,1)S(1)}, u32[]{:S(2)}, u32[]{:S(2)}) collective-permute-start(bf16[96,1024]{1,0:T(8,128)(2,1)S(1)} %get-tuple-element.57.refs_2_), channel_id=1, source_target_pairs={{0,16},{2,18},{4,20},{6,22},{8,24},{10,26},{12,28},{14,30},{16,0},... | collective-permute-start | bytes 589832 | tf_op jit(solution)/shard_map/ppermute | solution.py:32
  149.4 14.5 %collective-permute-start.32 = (bf16[96,1024]{1,0:T(8,128)(2,1)S(1)}, bf16[96,1024]{1,0:T(8,128)(2,1)S(1)}, u32[]{:S(2)}, u32[]{:S(2)}) collective-permute-start(bf16[96,1024]{1,0:T(8,128)(2,1)S(1)} %get-tuple-element.58), channel_id=1, source_target_pairs={{0,32},{2,34},{4,36},{6,38},{8,40},{10,42},{12,44},{14,46},{16,48}... | collective-permute-start | bytes 589832 | tf_op jit(solution)/shard_map/ppermute | solution.py:32
  152.9 11.1 %collective-permute-start.33 = (bf16[96,1024]{1,0:T(8,128)(2,1)S(1)}, bf16[96,1024]{1,0:T(8,128)(2,1)S(1)}, u32[]{:S(2)}, u32[]{:S(2)}) collective-permute-start(bf16[96,1024]{1,0:T(8,128)(2,1)S(1)} %get-tuple-element.59), channel_id=1, source_target_pairs={{0,48},{2,50},{4,52},{6,54},{8,56},{10,58},{12,60},{14,62},{16,32}... | collective-permute-start | bytes 589832 | tf_op jit(solution)/shard_map/ppermute | solution.py:32
  (25 other events, 187.3 us)

commit v4 on v3

--- a/solution.py
+++ b/solution.py
@@ -157,26 +157,34 @@
     return [got[k] for k in (1, 2, 3)]
 
 
-def backward_kernel(b0, b1, b2, b3, w_gate, w_up, out):
+def backward_kernel(*refs):
+    *blocks, w_gate, w_up, out = refs
     total = 0.0
     for i, w in enumerate((w_gate, w_up)):
-        left = jnp.concatenate([b[i] for b in (b0, b1, b2, b3)], axis=0)
+        left = jnp.concatenate([b[i] for b in blocks], axis=0)
         total += lax.dot_general(
             left, w[...], (((1,), (1,)), ((), ())), preferred_element_type=F32
         )
-    for k in range(4):
+    for k in range(len(blocks)):
         out[k] = total[k * ROWS : (k + 1) * ROWS]
 
 
-def backward(blocks, w_gate, w_up, flops=1):
-    outs = [shape(4, ROWS, WIDE, dtype=F32)]
-    return call(backward_kernel, [*blocks, w_gate, w_up], outs, 12, flops=flops)[0]
-
-
-def join_kernel(y_ref, mine, theirs, *outs):
+def backward(blocks, w_gate, w_up, flops=1, later_than=()):
+    outs = [shape(len(blocks), ROWS, WIDE, dtype=F32)]
+    return call(backward_kernel, [*blocks, w_gate, w_up], outs, 12, later_than, flops=flops)[0]
+
+
+def join_kernel(y_ref, mine, low, high, *outs):
     for j, out in enumerate(outs):
         slot = y_ref[0] ^ j
-        out[...] = (mine[slot] + theirs[slot]).astype(out.dtype)
+
+        @pl.when(slot < 2)
+        def _():
+            out[...] = (mine[slot] + low[slot]).astype(out.dtype)
+
+        @pl.when(slot >= 2)
+        def _():
+            out[...] = (mine[slot] + high[slot - 2]).astype(out.dtype)
 
 
 def sum_kernel(own, p1, p2, p3, *outs):
@@ -191,7 +199,7 @@
 
 def join_step(y, mine, theirs):
     outs = [shape(ROWS, WIDE, dtype=F32)] + [shape(ROWS, WIDE)] * 3
-    return call(join_kernel, [mine, theirs], outs, 12, (), y)
+    return call(join_kernel, [mine, *theirs], outs, 12, (), y)
 
 
 def sum_step(total, parts, later_than):
@@ -264,7 +272,9 @@
     grads2, hidden2 = grads_step(total2, half2, blocks1[1:])
     blocks2 = [grads2] + swap_all_y([grads2] * 3)
     mine = backward(blocks1, w_gate, w_up, 2 * 2 * 4 * ROWS * WIDE * HID)
-    theirs = swap_core(backward(blocks2, w_gate, w_up))
+    low = backward(blocks2[:2], w_gate, w_up)
+    high = backward(blocks2[2:], w_gate, w_up, 1, [low])
+    theirs = [swap_core(low), swap_core(high)]
     (hidden,) = call(stack_kernel, [hidden1, hidden2], [shape(2, ROWS, HID)], 4, blocks2[1:])
     hiddens = [hidden] + swap_all_y([hidden] * 3)
 
@@ -274,7 +284,7 @@
     outs = [shape(8 * ROWS, WIDE)] * 2
     xs, gs = call(tokens_kernel, [tokens1, tokens2], outs, 16, parts[:1])
     grad_gate = dot(xs, gate_grad)
-    sums = sum_step(total, parts, [grad_gate[:16, :128], *hiddens[1:]])
+    sums = sum_step(total, parts, [grad_gate[:16, :128], *hiddens[1:3]])
     grad_up = dot(xs, rows_step(1, blocks, 1, sums[:1]))
     (hidden,) = call(hidden_rows_kernel, hiddens, [shape(8 * ROWS, HID)], 12, sums[:1])
     got = [swap_z(part, j + 1) for j, part in enumerate(sums[1:])]

time: 175 us -> 173 us (0.989)
  waiting for transfers between devices: 84.7 us -> 77.9 us
  starting transfers between devices: 64.7 us -> 68.8 us
    ppermute x40 -> x41, waiting for transfers between devices: 84.7 us -> 77.9 us  [swap(): return lax.ppermute(value, AXES, pairs)]
    ppermute x40 -> x41, starting transfers between devices: 64.7 us -> 68.8 us  [swap(): return lax.ppermute(value, AXES, pairs)]
    pallas_call x20 -> x21, Pallas kernels: 11.8 us -> 12.7 us  [call(): pl.pallas_call(run, out_shape=outs, in_specs=[SMEM] * first + [VMEM] * (l...]
  transfers between devices with their start and end apart: 40 -> 41, of which waited for: 21 -> 21; matrix products, arithmetic and copies ran while one was open for 4% -> 4% of each run, Pallas kernels for 5% -> 6%
where the time goes in v4:
time: 173 us
  waiting for transfers between devices  77.9 us (45%)
  starting transfers between devices  68.8 us (40%)
  Pallas kernels  12.7 us (7%)
  matrix products  7.77 us (4%)
  local copies, waits for them, and re-layouts  4.53 us (3%)
    ppermute x41, waiting for transfers between devices, swap(): return lax.ppermute(value, AXES, pairs)  77.9 us
    ppermute x41, starting transfers between devices, swap(): return lax.ppermute(value, AXES, pairs)  68.8 us
    pallas_call x21, Pallas kernels, call(): pl.pallas_call(run, out_shape=outs, in_specs=[SMEM] * first + [VMEM] * (l...  12.7 us
    dot_general x3, matrix products, dot(): lax.dot_general(left, right, (((0,), (0,)), ((), ())), preferred_element_...  7.77 us
    unnamed x18, local copies, waits for them, and re-layouts  4.52 us
  transfers between devices with their start and end apart: 41, of which 21 were waited for; matrix products, arithmetic and copies ran while one was open for 4% of the time, Pallas kernels for 6%

profile of v4, /device:TPU:1, one launch (start us, length us, event | category | flops | bytes accessed | tf_op | source)
XLA Modules:
  0.0 172.7 jit_solution(9085347709159034268)
XLA Ops:
  3.2 3.0 %collective-permute-start.1 = (bf16[24,1024]{1,0:T(8,128)(2,1)}, bf16[24,1024]{1,0:T(8,128)(2,1)S(1)}, u32[]{:S(2)}, u32[]{:S(2)}) collective-permute-start(bf16[24,1024]{1,0:T(8,128)(2,1)} %refs_0_.4), channel_id=1, source_target_pairs={{0,128},{2,130},{4,132},{6,134},{8,136},{10,138},{12,140},{14,142}... | collective-permute-start | bytes 147464 | tf_op jit(solution)/shard_map/ppermute | solution.py:32
  20.4 2.9 %collective-permute-done.8.refs_3_ = bf16[24,1024]{1,0:T(8,128)(2,1)S(1)} collective-permute-done((bf16[24,1024]{1,0:T(8,128)(2,1)S(1)}, bf16[24,1024]{1,0:T(8,128)(2,1)S(1)}, u32[]{:S(2)}, u32[]{:S(2)}) %collective-permute-start.8) | collective-permute-done | bytes 49184 | tf_op jit(solution)/shard_map/ppermute | solution.py:32
  34.7 3.4 %collective-permute-done.13.refs_3_ = bf16[96,1024]{1,0:T(8,128)(2,1)S(1)} collective-permute-done((bf16[96,1024]{1,0:T(8,128)(2,1)S(1)}, bf16[96,1024]{1,0:T(8,128)(2,1)S(1)}, u32[]{:S(2)}, u32[]{:S(2)}) %collective-permute-start.13) | collective-permute-done | bytes 196640 | tf_op jit(solution)/shard_map/ppermute | solution.py:32
  40.2 3.4 %collective-permute-done.10.refs_8_.refs_2_ = bf16[2,96,896]{2,1,0:T(8,128)(2,1)S(1)} collective-permute-done((bf16[2,96,896]{2,1,0:T(8,128)(2,1)S(1)}, bf16[2,96,896]{2,1,0:T(8,128)(2,1)S(1)}, u32[]{:S(2)}, u32[]{:S(2)}) %collective-permute-start.10) | collective-permute-done | bytes 344096 | tf_op jit(solution)/shard_map/ppermute | solution.py:32
  45.7 6.7 %collective-permute-start.19 = (bf16[2,4,96,1024]{3,2,1,0:T(8,128)(2,1)S(1)}, bf16[2,4,96,1024]{3,2,1,0:T(8,128)(2,1)S(1)}, u32[]{:S(2)}, u32[]{:S(2)}) collective-permute-start(bf16[2,4,96,1024]{3,2,1,0:T(8,128)(2,1)S(1)} %get-tuple-element.47.refs_0_), channel_id=1, source_target_pairs={{0,8},{2,10},{4,12},{6,14},{8,0},{10,2},{12,4},{14,6},{16,24},{18,... | collective-permute-start | bytes 4718600 | tf_op jit(solution)/shard_map/ppermute | solution.py:32
  53.5 2.7 %collective-permute-start.17 = (bf16[1,96,896]{2,1,0:T(8,128)(2,1)S(1)}, bf16[1,96,896]{2,1,0:T(8,128)(2,1)S(1)}, u32[]{:S(2)}, u32[]{:S(2)}) collective-permute-start(bf16[1,96,896]{2,1,0:T(8,128)(2,1)S(1)} %get-tuple-element.44), channel_id=1, source_target_pairs={{0,6},{2,4},{4,2},{6,0},{8,14},{10,12},{12,10},{14,8},{16,22},{18,... | collective-permute-start | bytes 516104 | tf_op jit(solution)/shard_map/ppermute | solution.py:32
  60.1 2.7 %collective-permute-start.22 = (bf16[3,96,896]{2,1,0:T(8,128)(2,1)S(1)}, bf16[3,96,896]{2,1,0:T(8,128)(2,1)S(1)}, u32[]{:S(2)}, u32[]{:S(2)}) collective-permute-start(bf16[3,96,896]{2,1,0:T(8,128)(2,1)S(1)} %get-tuple-element.51), channel_id=1, source_target_pairs={{0,6},{2,4},{4,2},{6,0},{8,14},{10,12},{12,10},{14,8},{16,22},{18,... | collective-permute-start | bytes 1548296 | tf_op jit(solution)/shard_map/ppermute | solution.py:32
  64.3 5.3 %collective-permute-start.18 = (bf16[3,96,896]{2,1,0:T(8,128)(2,1)S(1)}, bf16[3,96,896]{2,1,0:T(8,128)(2,1)S(1)}, u32[]{:S(2)}, u32[]{:S(2)}) collective-permute-start(bf16[3,96,896]{2,1,0:T(8,128)(2,1)S(1)} %get-tuple-element.46.refs_4_), channel_id=1, source_target_pairs={{0,1},{2,3},{4,5},{6,7},{8,9},{10,11},{12,13},{14,15},{16,17},{18,... | collective-permute-start | bytes 1548296 | tf_op jit(solution)/shard_map/ppermute | solution.py:32
  69.5 3.4 %collective-permute-done.20.refs_1_ = bf16[3,96,896]{2,1,0:T(8,128)(2,1)S(1)} collective-permute-done((bf16[3,96,896]{2,1,0:T(8,128)(2,1)S(1)}, bf16[3,96,896]{2,1,0:T(8,128)(2,1)S(1)}, u32[]{:S(2)}, u32[]{:S(2)}) %collective-permute-start.20) | collective-permute-done | bytes 516128 | tf_op jit(solution)/shard_map/ppermute | solution.py:32
  72.9 10.8 %collective-permute-done.21.refs_2_ = bf16[3,96,896]{2,1,0:T(8,128)(2,1)S(1)} collective-permute-done((bf16[3,96,896]{2,1,0:T(8,128)(2,1)S(1)}, bf16[3,96,896]{2,1,0:T(8,128)(2,1)S(1)}, u32[]{:S(2)}, u32[]{:S(2)}) %collective-permute-start.21) | collective-permute-done | bytes 516128 | tf_op jit(solution)/shard_map/ppermute | solution.py:32
  86.0 5.3 %collective-permute-start.26 = (bf16[3,96,896]{2,1,0:T(8,128)(2,1)S(1)}, bf16[3,96,896]{2,1,0:T(8,128)(2,1)S(1)}, u32[]{:S(2)}, u32[]{:S(2)}) collective-permute-start(bf16[3,96,896]{2,1,0:T(8,128)(2,1)S(1)} %get-tuple-element.52.refs_2_), channel_id=1, source_target_pairs={{0,1},{2,3},{4,5},{6,7},{8,9},{10,11},{12,13},{14,15},{16,17},{18,... | collective-permute-start | bytes 1548296 | tf_op jit(solution)/shard_map/ppermute | solution.py:32
  91.6 3.8 %collective-permute-start.24 = (bf16[2,96,896]{2,1,0:T(8,128)(2,1)S(1)}, bf16[2,96,896]{2,1,0:T(8,128)(2,1)S(1)}, u32[]{:S(2)}, u32[]{:S(2)}) collective-permute-start(bf16[2,96,896]{2,1,0:T(8,128)(2,1)S(1)} %get-tuple-element.53.refs_0_), channel_id=1, source_target_pairs={{0,4},{2,6},{4,0},{6,2},{8,12},{10,14},{12,8},{14,10},{16,20},{18,... | collective-permute-start | bytes 1032200 | tf_op jit(solution)/shard_map/ppermute | solution.py:32
  95.5 3.8 %collective-permute-done.23.refs_1_.refs_2_ = bf16[2,96,896]{2,1,0:T(8,128)(2,1)S(1)} collective-permute-done((bf16[2,96,896]{2,1,0:T(8,128)(2,1)S(1)}, bf16[2,96,896]{2,1,0:T(8,128)(2,1)S(1)}, u32[]{:S(2)}, u32[]{:S(2)}) %collective-permute-start.23) | collective-permute-done | bytes 344096 | tf_op jit(solution)/shard_map/ppermute | solution.py:32
  99.3 9.8 %collective-permute-done.24.refs_2_.refs_3_ = bf16[2,96,896]{2,1,0:T(8,128)(2,1)S(1)} collective-permute-done((bf16[2,96,896]{2,1,0:T(8,128)(2,1)S(1)}, bf16[2,96,896]{2,1,0:T(8,128)(2,1)S(1)}, u32[]{:S(2)}, u32[]{:S(2)}) %collective-permute-start.24) | collective-permute-done | bytes 344096 | tf_op jit(solution)/shard_map/ppermute | solution.py:32
  109.1 8.6 %collective-permute-done.26.refs_1_ = bf16[3,96,896]{2,1,0:T(8,128)(2,1)S(1)} collective-permute-done((bf16[3,96,896]{2,1,0:T(8,128)(2,1)S(1)}, bf16[3,96,896]{2,1,0:T(8,128)(2,1)S(1)}, u32[]{:S(2)}, u32[]{:S(2)}) %collective-permute-start.26) | collective-permute-done | bytes 516128 | tf_op jit(solution)/shard_map/ppermute | solution.py:32
  118.1 3.8 %collective-permute-start.29 = (bf16[2,96,896]{2,1,0:T(8,128)(2,1)S(1)}, bf16[2,96,896]{2,1,0:T(8,128)(2,1)S(1)}, u32[]{:S(2)}, u32[]{:S(2)}) collective-permute-start(bf16[2,96,896]{2,1,0:T(8,128)(2,1)S(1)} %get-tuple-element.55.refs_0_.refs_4_), channel_id=1, source_target_pairs={{0,4},{2,6},{4,0},{6,2},{8,12},{10,14},{12,8},{14,10},{16,20},{18,... | collective-permute-start | bytes 1032200 | tf_op jit(solution)/shard_map/ppermute | solution.py:32
  121.9 4.9 %collective-permute-done.27.refs_1_.refs_5_.refs_2_ = bf16[2,96,896]{2,1,0:T(8,128)(2,1)S(1)} collective-permute-done((bf16[2,96,896]{2,1,0:T(8,128)(2,1)S(1)}, bf16[2,96,896]{2,1,0:T(8,128)(2,1)S(1)}, u32[]{:S(2)}, u32[]{:S(2)}) %collective-permute-start.27) | collective-permute-done | bytes 344096 | tf_op jit(solution)/shard_map/ppermute | solution.py:32
  128.2 3.2 %collective-permute-start.28 = (f32[2,96,1024]{2,1,0:T(8,128)S(1)}, f32[2,96,1024]{2,1,0:T(8,128)S(1)}, u32[]{:S(2)}, u32[]{:S(2)}) collective-permute-start(f32[2,96,1024]{2,1,0:T(8,128)S(1)} %shard_map.95.refs_4_), channel_id=1, source_target_pairs={{0,8},{2,10},{4,12},{6,14},{8,0},{10,2},{12,4},{14,6},{16,24},{18,... | collective-permute-start | bytes 2359304 | tf_op jit(solution)/shard_map/ppermute | solution.py:32
  131.3 5.3 %collective-permute-done.29.refs_0_.refs_6_.refs_3_ = bf16[2,96,896]{2,1,0:T(8,128)(2,1)S(1)} collective-permute-done((bf16[2,96,896]{2,1,0:T(8,128)(2,1)S(1)}, bf16[2,96,896]{2,1,0:T(8,128)(2,1)S(1)}, u32[]{:S(2)}, u32[]{:S(2)}) %collective-permute-start.29) | collective-permute-done | bytes 344096 | tf_op jit(solution)/shard_map/ppermute | solution.py:32
  146.4 3.7 %collective-permute-start.34 = (bf16[96,1024]{1,0:T(8,128)(2,1)S(1)}, bf16[96,1024]{1,0:T(8,128)(2,1)S(1)}, u32[]{:S(2)}, u32[]{:S(2)}) collective-permute-start(bf16[96,1024]{1,0:T(8,128)(2,1)S(1)} %get-tuple-element.59), channel_id=1, source_target_pairs={{0,48},{2,50},{4,52},{6,54},{8,56},{10,58},{12,60},{14,62},{16,32}... | collective-permute-start | bytes 589832 | tf_op jit(solution)/shard_map/ppermute | solution.py:32
  154.9 6.5 %collective-permute-done.36.refs_6_.refs_2_ = bf16[2,96,896]{2,1,0:T(8,128)(2,1)S(1)} collective-permute-done((bf16[2,96,896]{2,1,0:T(8,128)(2,1)S(1)}, bf16[2,96,896]{2,1,0:T(8,128)(2,1)S(1)}, u32[]{:S(2)}, u32[]{:S(2)}) %collective-permute-start.36) | collective-permute-done | bytes 344096 | tf_op jit(solution)/shard_map/ppermute | solution.py:32
  161.7 3.4 %collective-permute-start.39 = (f32[24,1024]{1,0:T(8,128)S(1)}, f32[24,1024]{1,0:T(8,128)S(1)}, u32[]{:S(2)}, u32[]{:S(2)}) collective-permute-start(f32[24,1024]{1,0:T(8,128)S(1)} %get-tuple-element.66), channel_id=1, source_target_pairs={{0,192},{2,194},{4,196},{6,198},{8,200},{10,202},{12,204},{14,206}... | collective-permute-start | bytes 294920 | tf_op jit(solution)/shard_map/ppermute | solution.py:32
  165.3 3.1 %convolution_convert_fusion.1 = bf16[1024,896]{1,0:T(8,128)(2,1)} fusion(bf16[768,1024]{1,0:T(8,128)(2,1)S(1)} %get-tuple-element.60, bf16[768,896]{1,0:T(8,128)(2,1)S(1)} %shard_map.103), kind=kOutput, calls=%fused_computation.1 | convolution fusion | flops 1410203648 | bytes 4784128 | tf_op jit(solution)/shard_map/dot_general | solution.py:242
  169.2 2.9 %convolution_convert_fusion = bf16[896,1024]{1,0:T(8,128)(2,1)} fusion(bf16[768,896]{1,0:T(8,128)(2,1)S(1)} %shard_map.104, bf16[768,1024]{1,0:T(8,128)(2,1)S(1)} %get-tuple-element.67), kind=kOutput, calls=%fused_computation | convolution fusion | flops 1410203648 | bytes 4784128 | tf_op jit(solution)/shard_map/dot_general | solution.py:242
  (101 shorter events, 59.5 us)
Async XLA Ops:
  11.2 12.4 %collective-permute-start.3 = (bf16[96,1024]{1,0:T(8,128)(2,1)S(1)}, bf16[96,1024]{1,0:T(8,128)(2,1)S(1)}, u32[]{:S(2)}, u32[]{:S(2)}) collective-permute-start(bf16[96,1024]{1,0:T(8,128)(2,1)S(1)} %shard_map.85.refs_1_), channel_id=1, source_target_pairs={{0,16},{2,18},{4,20},{6,22},{8,24},{10,26},{12,28},{14,30},{16,0},... | collective-permute-start | bytes 589832 | tf_op jit(solution)/shard_map/ppermute | solution.py:32
  12.5 11.1 %collective-permute-start.4 = (bf16[96,1024]{1,0:T(8,128)(2,1)S(1)}, bf16[96,1024]{1,0:T(8,128)(2,1)S(1)}, u32[]{:S(2)}, u32[]{:S(2)}) collective-permute-start(bf16[96,1024]{1,0:T(8,128)(2,1)S(1)} %shard_map.85.refs_1_), channel_id=1, source_target_pairs={{0,32},{2,34},{4,36},{6,38},{8,40},{10,42},{12,44},{14,46},{16,48}... | collective-permute-start | bytes 589832 | tf_op jit(solution)/shard_map/ppermute | solution.py:32
  23.4 10.9 %collective-permute-start.12 = (bf16[96,1024]{1,0:T(8,128)(2,1)S(1)}, bf16[96,1024]{1,0:T(8,128)(2,1)S(1)}, u32[]{:S(2)}, u32[]{:S(2)}) collective-permute-start(bf16[96,1024]{1,0:T(8,128)(2,1)S(1)} %shard_map.86.refs_7_.refs_1_), channel_id=1, source_target_pairs={{0,16},{2,18},{4,20},{6,22},{8,24},{10,26},{12,28},{14,30},{16,0},... | collective-permute-start | bytes 589832 | tf_op jit(solution)/shard_map/ppermute | solution.py:32
  28.1 12.1 %collective-permute-start.9 = (bf16[2,96,896]{2,1,0:T(8,128)(2,1)S(1)}, bf16[2,96,896]{2,1,0:T(8,128)(2,1)S(1)}, u32[]{:S(2)}, u32[]{:S(2)}) collective-permute-start(bf16[2,96,896]{2,1,0:T(8,128)(2,1)S(1)} %get-tuple-element.37), channel_id=1, source_target_pairs={{0,2},{2,0},{4,6},{6,4},{8,10},{10,8},{12,14},{14,12},{16,18},{18,... | collective-permute-start | bytes 1032200 | tf_op jit(solution)/shard_map/ppermute | solution.py:32
  29.5 14.1 %collective-permute-start.10 = (bf16[2,96,896]{2,1,0:T(8,128)(2,1)S(1)}, bf16[2,96,896]{2,1,0:T(8,128)(2,1)S(1)}, u32[]{:S(2)}, u32[]{:S(2)}) collective-permute-start(bf16[2,96,896]{2,1,0:T(8,128)(2,1)S(1)} %get-tuple-element.38), channel_id=1, source_target_pairs={{0,4},{2,6},{4,0},{6,2},{8,12},{10,14},{12,8},{14,10},{16,20},{18,... | collective-permute-start | bytes 1032200 | tf_op jit(solution)/shard_map/ppermute | solution.py:32
  32.1 12.5 %collective-permute-start.11 = (bf16[2,96,896]{2,1,0:T(8,128)(2,1)S(1)}, bf16[2,96,896]{2,1,0:T(8,128)(2,1)S(1)}, u32[]{:S(2)}, u32[]{:S(2)}) collective-permute-start(bf16[2,96,896]{2,1,0:T(8,128)(2,1)S(1)} %get-tuple-element.39), channel_id=1, source_target_pairs={{0,6},{2,4},{4,2},{6,0},{8,14},{10,12},{12,10},{14,8},{16,22},{18,... | collective-permute-start | bytes 1032200 | tf_op jit(solution)/shard_map/ppermute | solution.py:32
  45.7 10.6 %collective-permute-start.19 = (bf16[2,4,96,1024]{3,2,1,0:T(8,128)(2,1)S(1)}, bf16[2,4,96,1024]{3,2,1,0:T(8,128)(2,1)S(1)}, u32[]{:S(2)}, u32[]{:S(2)}) collective-permute-start(bf16[2,4,96,1024]{3,2,1,0:T(8,128)(2,1)S(1)} %get-tuple-element.47.refs_0_), channel_id=1, source_target_pairs={{0,8},{2,10},{4,12},{6,14},{8,0},{10,2},{12,4},{14,6},{16,24},{18,... | collective-permute-start | bytes 4718600 | tf_op jit(solution)/shard_map/ppermute | solution.py:32
  53.5 10.5 %collective-permute-start.17 = (bf16[1,96,896]{2,1,0:T(8,128)(2,1)S(1)}, bf16[1,96,896]{2,1,0:T(8,128)(2,1)S(1)}, u32[]{:S(2)}, u32[]{:S(2)}) collective-permute-start(bf16[1,96,896]{2,1,0:T(8,128)(2,1)S(1)} %get-tuple-element.44), channel_id=1, source_target_pairs={{0,6},{2,4},{4,2},{6,0},{8,14},{10,12},{12,10},{14,8},{16,22},{18,... | collective-permute-start | bytes 516104 | tf_op jit(solution)/shard_map/ppermute | solution.py:32
  58.9 14.1 %collective-permute-start.20 = (bf16[3,96,896]{2,1,0:T(8,128)(2,1)S(1)}, bf16[3,96,896]{2,1,0:T(8,128)(2,1)S(1)}, u32[]{:S(2)}, u32[]{:S(2)}) collective-permute-start(bf16[3,96,896]{2,1,0:T(8,128)(2,1)S(1)} %get-tuple-element.49), channel_id=1, source_target_pairs={{0,2},{2,0},{4,6},{6,4},{8,10},{10,8},{12,14},{14,12},{16,18},{18,... | collective-permute-start | bytes 1548296 | tf_op jit(solution)/shard_map/ppermute | solution.py:32
  59.0 24.8 %collective-permute-start.21 = (bf16[3,96,896]{2,1,0:T(8,128)(2,1)S(1)}, bf16[3,96,896]{2,1,0:T(8,128)(2,1)S(1)}, u32[]{:S(2)}, u32[]{:S(2)}) collective-permute-start(bf16[3,96,896]{2,1,0:T(8,128)(2,1)S(1)} %get-tuple-element.50), channel_id=1, source_target_pairs={{0,4},{2,6},{4,0},{6,2},{8,12},{10,14},{12,8},{14,10},{16,20},{18,... | collective-permute-start | bytes 1548296 | tf_op jit(solution)/shard_map/ppermute | solution.py:32
  60.1 25.6 %collective-permute-start.22 = (bf16[3,96,896]{2,1,0:T(8,128)(2,1)S(1)}, bf16[3,96,896]{2,1,0:T(8,128)(2,1)S(1)}, u32[]{:S(2)}, u32[]{:S(2)}) collective-permute-start(bf16[3,96,896]{2,1,0:T(8,128)(2,1)S(1)} %get-tuple-element.51), channel_id=1, source_target_pairs={{0,6},{2,4},{4,2},{6,0},{8,14},{10,12},{12,10},{14,8},{16,22},{18,... | collective-permute-start | bytes 1548296 | tf_op jit(solution)/shard_map/ppermute | solution.py:32
  64.3 27.0 %collective-permute-start.18 = (bf16[3,96,896]{2,1,0:T(8,128)(2,1)S(1)}, bf16[3,96,896]{2,1,0:T(8,128)(2,1)S(1)}, u32[]{:S(2)}, u32[]{:S(2)}) collective-permute-start(bf16[3,96,896]{2,1,0:T(8,128)(2,1)S(1)} %get-tuple-element.46.refs_4_), channel_id=1, source_target_pairs={{0,1},{2,3},{4,5},{6,7},{8,9},{10,11},{12,13},{14,15},{16,17},{18,... | collective-permute-start | bytes 1548296 | tf_op jit(solution)/shard_map/ppermute | solution.py:32
  86.0 31.7 %collective-permute-start.26 = (bf16[3,96,896]{2,1,0:T(8,128)(2,1)S(1)}, bf16[3,96,896]{2,1,0:T(8,128)(2,1)S(1)}, u32[]{:S(2)}, u32[]{:S(2)}) collective-permute-start(bf16[3,96,896]{2,1,0:T(8,128)(2,1)S(1)} %get-tuple-element.52.refs_2_), channel_id=1, source_target_pairs={{0,1},{2,3},{4,5},{6,7},{8,9},{10,11},{12,13},{14,15},{16,17},{18,... | collective-permute-start | bytes 1548296 | tf_op jit(solution)/shard_map/ppermute | solution.py:32
  91.6 17.5 %collective-permute-start.24 = (bf16[2,96,896]{2,1,0:T(8,128)(2,1)S(1)}, bf16[2,96,896]{2,1,0:T(8,128)(2,1)S(1)}, u32[]{:S(2)}, u32[]{:S(2)}) collective-permute-start(bf16[2,96,896]{2,1,0:T(8,128)(2,1)S(1)} %get-tuple-element.53.refs_0_), channel_id=1, source_target_pairs={{0,4},{2,6},{4,0},{6,2},{8,12},{10,14},{12,8},{14,10},{16,20},{18,... | collective-permute-start | bytes 1032200 | tf_op jit(solution)/shard_map/ppermute | solution.py:32
  95.5 13.6 %collective-permute-start.25 = (bf16[2,96,896]{2,1,0:T(8,128)(2,1)S(1)}, bf16[2,96,896]{2,1,0:T(8,128)(2,1)S(1)}, u32[]{:S(2)}, u32[]{:S(2)}) collective-permute-start(bf16[2,96,896]{2,1,0:T(8,128)(2,1)S(1)} %get-tuple-element.53.refs_0_), channel_id=1, source_target_pairs={{0,6},{2,4},{4,2},{6,0},{8,14},{10,12},{12,10},{14,8},{16,22},{18,... | collective-permute-start | bytes 1032200 | tf_op jit(solution)/shard_map/ppermute | solution.py:32
  118.1 18.5 %collective-permute-start.29 = (bf16[2,96,896]{2,1,0:T(8,128)(2,1)S(1)}, bf16[2,96,896]{2,1,0:T(8,128)(2,1)S(1)}, u32[]{:S(2)}, u32[]{:S(2)}) collective-permute-start(bf16[2,96,896]{2,1,0:T(8,128)(2,1)S(1)} %get-tuple-element.55.refs_0_.refs_4_), channel_id=1, source_target_pairs={{0,4},{2,6},{4,0},{6,2},{8,12},{10,14},{12,8},{14,10},{16,20},{18,... | collective-permute-start | bytes 1032200 | tf_op jit(solution)/shard_map/ppermute | solution.py:32
  121.9 16.7 %collective-permute-start.30 = (bf16[2,96,896]{2,1,0:T(8,128)(2,1)S(1)}, bf16[2,96,896]{2,1,0:T(8,128)(2,1)S(1)}, u32[]{:S(2)}, u32[]{:S(2)}) collective-permute-start(bf16[2,96,896]{2,1,0:T(8,128)(2,1)S(1)} %get-tuple-element.55.refs_0_.refs_4_), channel_id=1, source_target_pairs={{0,6},{2,4},{4,2},{6,0},{8,14},{10,12},{12,10},{14,8},{16,22},{18,... | collective-permute-start | bytes 1032200 | tf_op jit(solution)/shard_map/ppermute | solution.py:32
  128.2 17.7 %collective-permute-start.28 = (f32[2,96,1024]{2,1,0:T(8,128)S(1)}, f32[2,96,1024]{2,1,0:T(8,128)S(1)}, u32[]{:S(2)}, u32[]{:S(2)}) collective-permute-start(f32[2,96,1024]{2,1,0:T(8,128)S(1)} %shard_map.95.refs_4_), channel_id=1, source_target_pairs={{0,8},{2,10},{4,12},{6,14},{8,0},{10,2},{12,4},{14,6},{16,24},{18,... | collective-permute-start | bytes 2359304 | tf_op jit(solution)/shard_map/ppermute | solution.py:32
  144.6 16.8 %collective-permute-start.36 = (bf16[2,96,896]{2,1,0:T(8,128)(2,1)S(1)}, bf16[2,96,896]{2,1,0:T(8,128)(2,1)S(1)}, u32[]{:S(2)}, u32[]{:S(2)}) collective-permute-start(bf16[2,96,896]{2,1,0:T(8,128)(2,1)S(1)} %shard_map.100.refs_0_), channel_id=1, source_target_pairs={{0,4},{2,6},{4,0},{6,2},{8,12},{10,14},{12,8},{14,10},{16,20},{18,... | collective-permute-start | bytes 1032200 | tf_op jit(solution)/shard_map/ppermute | solution.py:32
  146.2 15.3 %collective-permute-start.32 = (bf16[96,1024]{1,0:T(8,128)(2,1)S(1)}, bf16[96,1024]{1,0:T(8,128)(2,1)S(1)}, u32[]{:S(2)}, u32[]{:S(2)}) collective-permute-start(bf16[96,1024]{1,0:T(8,128)(2,1)S(1)} %get-tuple-element.57.refs_2_), channel_id=1, source_target_pairs={{0,16},{2,18},{4,20},{6,22},{8,24},{10,26},{12,28},{14,30},{16,0},... | collective-permute-start | bytes 589832 | tf_op jit(solution)/shard_map/ppermute | solution.py:32
  146.3 15.2 %collective-permute-start.33 = (bf16[96,1024]{1,0:T(8,128)(2,1)S(1)}, bf16[96,1024]{1,0:T(8,128)(2,1)S(1)}, u32[]{:S(2)}, u32[]{:S(2)}) collective-permute-start(bf16[96,1024]{1,0:T(8,128)(2,1)S(1)} %get-tuple-element.58), channel_id=1, source_target_pairs={{0,32},{2,34},{4,36},{6,38},{8,40},{10,42},{12,44},{14,46},{16,48}... | collective-permute-start | bytes 589832 | tf_op jit(solution)/shard_map/ppermute | solution.py:32
  146.4 15.1 %collective-permute-start.34 = (bf16[96,1024]{1,0:T(8,128)(2,1)S(1)}, bf16[96,1024]{1,0:T(8,128)(2,1)S(1)}, u32[]{:S(2)}, u32[]{:S(2)}) collective-permute-start(bf16[96,1024]{1,0:T(8,128)(2,1)S(1)} %get-tuple-element.59), channel_id=1, source_target_pairs={{0,48},{2,50},{4,52},{6,54},{8,56},{10,58},{12,60},{14,62},{16,32}... | collective-permute-start | bytes 589832 | tf_op jit(solution)/shard_map/ppermute | solution.py:32
  154.3 14.8 %collective-permute-start.40 = (bf16[2,96,896]{2,1,0:T(8,128)(2,1)S(1)}, bf16[2,96,896]{2,1,0:T(8,128)(2,1)S(1)}, u32[]{:S(2)}, u32[]{:S(2)}) collective-permute-start(bf16[2,96,896]{2,1,0:T(8,128)(2,1)S(1)} %shard_map.100.refs_0_), channel_id=1, source_target_pairs={{0,6},{2,4},{4,2},{6,0},{8,14},{10,12},{12,10},{14,8},{16,22},{18,... | collective-permute-start | bytes 1032200 | tf_op jit(solution)/shard_map/ppermute | solution.py:32
  161.5 10.5 %collective-permute-start.37 = (f32[24,1024]{1,0:T(8,128)S(1)}, f32[24,1024]{1,0:T(8,128)S(1)}, u32[]{:S(2)}, u32[]{:S(2)}) collective-permute-start(f32[24,1024]{1,0:T(8,128)S(1)} %get-tuple-element.64), channel_id=1, source_target_pairs={{0,64},{2,66},{4,68},{6,70},{8,72},{10,74},{12,76},{14,78},{16,80}... | collective-permute-start | bytes 294920 | tf_op jit(solution)/shard_map/ppermute | solution.py:32
  (26 other events, 197.1 us)
